TPU v7x, 256 devices: a whole 4x4x8 slice. The times are simulated.
256 devices in a mesh: gx: 32 (over y, z_hi, x), gy: 8 (over z_lo, core).
Axes of the slice: x: 4, y: 4, z: 8 (z_hi: 2, z_lo: 4; z = z_hi * 4 + z_lo), core: 2. Of those that a mesh axis runs over, the one named last changes fastest.
Arguments:
- species_field: float32 [256, 1024, 1024], P(None, 'gx', 'gy'), may hold values from -6 to 6
- basis_one: float32 [1024, 256], replicated, may hold values from -0.1875 to 0.1875
- basis_two: float32 [1024, 256], replicated, may hold values from -0.1875 to 0.1875
Outputs:
- core_tensor: float32 [256, 256, 256], P('gx', 'gy')
All inputs are finite; a program needn't handle non-finite values.
Results may differ from a plain program's by a relative error of at most 0.000084.
Values sent between devices are 32-bit elements; how exact they have to be, the bound alone decides.
No kernel may reach another device: no remote copies, remote signals or barrier semaphores. Data moves between devices by JAX's collectives and lax.ppermute only.
A program may use at most 128 MiB of HBM per device.

v0:
```python
import jax
import jax.numpy as jnp
from jax import lax
from jax.sharding import PartitionSpec as P


def on_device(species_field, basis_one, basis_two):
    slab_depth, rows_one, cols_two = species_field.shape
    regrouped = lax.all_to_all(species_field, "gx", split_axis=0, concat_axis=1, tiled=True)
    reduced = jnp.einsum("kij,ir->krj", regrouped, basis_one, precision=lax.Precision.HIGHEST)
    start_two = lax.axis_index("gy") * cols_two
    local_two = lax.dynamic_slice_in_dim(basis_two, start_two, cols_two, 0)
    partial_core = jnp.einsum("krj,js->krs", reduced, local_two, precision=lax.Precision.HIGHEST)
    core_tensor = lax.psum_scatter(partial_core, "gy", scatter_dimension=1, tiled=True)
    return core_tensor


def solution(mesh):
    placed = (P(None, "gx", "gy"), P(), P())
    return jax.shard_map(
        on_device, mesh=mesh, in_specs=placed, out_specs=P("gx", "gy", None), check_vma=False
    )
```

profile of v0, /device:TPU:1, one launch (start us, length us, event | category | flops | bytes accessed | tf_op | source)
XLA Modules:
  0.0 173.2 jit_solution(3230890239431403577)
XLA Ops:
  6.5 0.0 copy-start
  6.5 14.8 %all-to-all-start = ((f32[256,32,128]{2,1,0:T(8,128)}), f32[256,32,128]{2,1,0:T(8,128)}, u32[]{:S(2)}, u32[]{:S(2)}) async-start(f32[256,32,128]{2,1,0:T(8,128)} %param.3), calls=%async_computation | async-start | bytes 8388608 | tf_op jit(solution)/shard_map/all_to_all | solution.py:9
  21.3 0.0 reduce-scatter.2.cloned.1.call-start
  21.4 69.8 %all-to-all-done = f32[256,32,128]{2,1,0:T(8,128)} async-done(((f32[256,32,128]{2,1,0:T(8,128)}), f32[256,32,128]{2,1,0:T(8,128)}, u32[]{:S(2)}, u32[]{:S(2)}) %all-to-all-start) | async-done | bytes 4194336 | tf_op jit(solution)/shard_map/all_to_all | solution.py:9
  91.1 0.0 copy-start.1
  91.1 2.9 %copy.4 = f32[8,32,32,128]{3,2,1,0:T(8,128)S(1)} copy(f32[8,32,32,128]{3,2,0,1:T(8,128)} %bitcast.2) | data formatting | bytes 8388608 | tf_op jit(solution)/shard_map/all_to_all | solution.py:9
  94.0 0.0 copy-done.1
  94.0 3.6 %convolution_bitcast_fusion = f32[8,256,128]{2,1,0:T(8,128)S(1)} fusion(f32[8,1024,128]{2,1,0:T(8,128)S(1)} %bitcast.14, f32[1024,256]{1,0:T(8,128)S(1)} %copy-done.1), kind=kOutput, calls=%fused_computation | convolution fusion | flops 3221225472 | bytes 6291456 | tf_op jit(solution)/shard_map/kij,ir->krj/dot_general | solution.py:10
  97.7 0.0 copy-done
  97.7 3.1 %fusion.1 = f32[8,256,256]{2,1,0:T(8,128)} fusion(f32[8,256,128]{2,1,0:T(8,128)S(1)} %convolution_bitcast_fusion, f32[1024,256]{1,0:T(8,128)S(1)} %copy-done, s32[]{:T(128)S(6)} %select_n.3), kind=kOutput, calls=%fused_computation.2 | convolution fusion | flops 805306368 | bytes 3276804 | tf_op jit(solution)/shard_map/krj,js->krs/dot_general | solution.py:13
  100.8 0.0 reduce-scatter.2.cloned.1.call-update
  100.9 65.5 %reduce-scatter.2.cloned.1.call-done = f32[8,32,256]{2,1,0:T(8,128)} async-done(((f32[8,256,256]{2,1,0:T(8,128)}), f32[8,32,256]{2,1,0:T(8,128)}) %reduce-scatter.2.cloned.1.call-update) | async-done | bytes 262160 | tf_op jit(solution)/shard_map/reduce_scatter | solution.py:14
Async XLA Ops:
  6.5 91.2 %copy-start = (f32[1024,256]{1,0:T(8,128)S(1)}, f32[1024,256]{1,0:T(8,128)}, u32[]{:S(2)}) copy-start(f32[1024,256]{1,0:T(8,128)} %param.5) | copy-start | bytes 3145732
  6.5 84.6 %all-to-all-start = ((f32[256,32,128]{2,1,0:T(8,128)}), f32[256,32,128]{2,1,0:T(8,128)}, u32[]{:S(2)}, u32[]{:S(2)}) async-start(f32[256,32,128]{2,1,0:T(8,128)} %param.3), calls=%async_computation | async-start | bytes 8388608 | tf_op jit(solution)/shard_map/all_to_all | solution.py:9
  21.3 145.0 %reduce-scatter.2.cloned.1.call-start = ((), (), s32[]{:S(2)}) async-start(), calls=%async_computation.2 | async-start | bytes 2359296 | tf_op jit(solution)/shard_map/reduce_scatter | solution.py:14
  91.1 2.9 %copy-start.1 = (f32[1024,256]{1,0:T(8,128)S(1)}, f32[1024,256]{1,0:T(8,128)}, u32[]{:S(2)}) copy-start(f32[1024,256]{1,0:T(8,128)} %param.4) | copy-start | bytes 3145732
Sparse Core Ops, SparseCore 0:
  101.0 65.3 reduce-scatter.1
where the time goes:
time: 175 us; the launch traced here: 173 us
  waiting for transfers between devices  135 us (77%)
  starting transfers between devices  14.8 us (8%)
  between operations  13.4 us (8%)
  matrix products  6.77 us (4%)
  local copies, waits for them, and re-layouts  2.9 us (2%)
    all_to_all x1, waiting for transfers between devices, on_device(): lax.all_to_all(species_field, 'gx', split_axis=0, concat_axis=1, tiled=True)  69.8 us
    reduce_scatter x1, waiting for transfers between devices, on_device(): lax.psum_scatter(partial_core, 'gy', scatter_dimension=1, tiled=True)  65.5 us
    all_to_all x1, starting transfers between devices, on_device(): lax.all_to_all(species_field, 'gx', split_axis=0, concat_axis=1, tiled=True)  14.8 us
    dot_general x1, matrix products, on_device(): jnp.einsum('kij,ir->krj', regrouped, basis_one, precision=lax.Precision.H...  3.64 us
  transfers between devices with their start and end apart: 2, of which 2 were waited for; matrix products, arithmetic and copies ran while one was open for 0% of the time, Pallas kernels for 0%

commit v1 on v0

v1 whole, which is shorter than its diff:
```python
import functools

import jax
import jax.numpy as jnp
from jax import lax
from jax.experimental import pallas as pl
from jax.experimental.pallas import tpu as pltpu
from jax.sharding import Mesh, PartitionSpec as P

AXES = ("y", "zh", "x", "zl", "c")
SIZES = (4, 2, 4, 4, 2)
CHUNKS = (2, 2)


def permuted(value, dz, flip):
    pairs = []
    for y in range(4):
        for z in range(8):
            for x in range(4):
                for c in range(2):
                    def at(z, c):
                        return (((y * 2 + z // 4) * 4 + x) * 4 + z % 4) * 2 + c
                    pairs.append((at(z, c), at((z + dz) % 8, c ^ flip)))
    return lax.ppermute(value, AXES, pairs)


def halves(value):
    high = lax.reduce_precision(value, 8, 7)
    return high.astype(jnp.bfloat16), (value - high).astype(jnp.bfloat16)


def dot3(left, right):
    dot = functools.partial(jnp.dot, preferred_element_type=jnp.float32)
    return dot(left[0], right[0]) + (dot(left[0], right[1]) + dot(left[1], right[0]))


def split(value):
    high = value.astype(jnp.bfloat16)
    return high, (value - high.astype(jnp.float32)).astype(jnp.bfloat16)


def contract_kernel(z_ref, x_ref, one_h, one_l, two_h, two_l, out_ref):
    block = jnp.concatenate([x_ref[:, c, 0, 0].reshape(512, 128) for c in range(2)], axis=1)
    reduced = dot3((one_h[...], one_l[...]), split(block))
    partial = dot3(split(reduced), (two_h[...], two_l[...]))
    zh, k = pl.program_id(0), pl.program_id(1)
    for zl in range(4):
        away = (zh * 4 + zl + 8 - z_ref[0]) % 8
        out_ref[away, k] = partial[zl * 64:(zl + 1) * 64]


def contract(position, received, one, two):
    n = received.shape[3]
    whole = lambda shape: pl.BlockSpec(shape, lambda zh, k, z: (0,) * len(shape))
    return pl.pallas_call(
        contract_kernel,
        grid_spec=pltpu.PrefetchScalarGridSpec(
            num_scalar_prefetch=1,
            grid=(2, n),
            in_specs=[pl.BlockSpec((16, 2, 1, 1, 32, 128), lambda zh, k, z: (0, 0, zh, k, 0, 0))]
            + [whole((256, 512))] * 2 + [whole((256, 256))] * 2,
            out_specs=whole((8, n, 64, 256)),
        ),
        out_shape=jax.ShapeDtypeStruct((8, n, 64, 256), jnp.float32),
        compiler_params=pltpu.CompilerParams(vmem_limit_bytes=24 << 20),
        cost_estimate=pl.CostEstimate(flops=n * 2 * 3 * 2 * 256 * 256 * 768, bytes_accessed=n * (3 << 20) // 2, transcendentals=0),
    )(position, received, *one, *two)


def scattered(parts, c):
    half = lambda v, which: lax.dynamic_slice_in_dim(v, which * 32, 32, 1)
    up = permuted(parts[4, :, :32], 1, 0)
    down = permuted(parts[4, :, 32:], -1, 0)
    swapped = permuted(half(parts[0], 1 - c), 0, 1)
    up = jnp.concatenate([parts[3, :, :32] + up, parts[3, :, 32:]], axis=1)
    down = jnp.concatenate([parts[5, :, :32], parts[5, :, 32:] + down], axis=1)
    up, down = permuted(up, 1, 0) + parts[2], permuted(down, -1, 0) + parts[6]
    up, down = permuted(up, 1, 0) + parts[1], permuted(down, -1, 0) + parts[7]
    own = half(parts[0], c) + permuted(half(up, c), 1, 0) + permuted(half(down, c), -1, 0)
    other = swapped + permuted(half(up, 1 - c), 1, 1) + permuted(half(down, 1 - c), -1, 1)
    return jnp.stack([jnp.where(c == 0, own, other), jnp.where(c == 0, other, own)])


def on_device(species_field, basis_one, basis_two):
    zh, zl, c = lax.axis_index("zh"), lax.axis_index("zl"), lax.axis_index("c")
    position = (zh * 4 + zl).astype(jnp.int32).reshape(1)
    rows = lax.dynamic_index_in_dim(basis_one.reshape(4, 2, 4, 32, 256), zh, 1, keepdims=False)
    one = halves(rows.reshape(512, 256).T)
    two = halves(lax.dynamic_slice_in_dim(basis_two, zl * 256, 256, 0))
    field = species_field.reshape(4, 2, 4, 2, 4, 32, 128)
    outs, start = [], 0
    for n in CHUNKS:
        piece = field[:, :, :, :, start:start + n].transpose(0, 2, 3, 1, 4, 5, 6).reshape(32 * 2 * n, 32, 128)
        moved = lax.all_to_all(piece, ("y", "x", "c"), split_axis=0, concat_axis=0, tiled=True)
        parts = contract(position, moved.reshape(16, 2, 2, n, 32, 128), one, two)
        outs.append(scattered(parts, c))
        start += n
    return jnp.concatenate(outs, axis=1).reshape(8, 32, 256)


def solution(mesh):
    fine = Mesh(mesh.devices.reshape(SIZES), AXES)
    placed = (P(None, ("y", "zh", "x"), ("zl", "c")), P(), P())
    return jax.shard_map(
        on_device, mesh=fine, in_specs=placed, out_specs=P(("y", "zh", "x"), ("zl", "c"), None), check_vma=False
    )
```

time: 175 us -> 127 us (0.73); the launches traced: 173 us -> 127 us
  waiting for transfers between devices: 135 us -> 47.6 us
  starting transfers between devices: 14.8 us -> 53.3 us
  between operations: 13.4 us -> 0.35 us
  local copies, waits for them, and re-layouts: 2.9 us -> 15 us
  Pallas kernels: 0 us -> 7.51 us
  matrix products: 6.77 us -> 0 us
  other arithmetic: 0 us -> 3.19 us
    reduce_scatter x1 -> x0, waiting for transfers between devices: 65.5 us -> none  [on_device(): lax.psum_scatter(partial_core, 'gy', scatter_dimension=1, tiled=True)]
    ppermute x0 -> x22, starting transfers between devices: none -> 38 us  [permuted(): return lax.ppermute(value, AXES, pairs)]
    all_to_all x1 -> x2, waiting for transfers between devices: 69.8 us -> 43.3 us  [on_device(): lax.all_to_all(piece, ('y', 'x', 'c'), split_axis=0, concat_axis=0, tiled...]
    transpose x0 -> x3, local copies, waits for them, and re-layouts: none -> 9.09 us  [on_device(): field[:, :, :, :, start:start + n].transpose(0, 2, 3, 1, 4, 5, 6)]
    pallas_call x0 -> x2, Pallas kernels: none -> 7.51 us  [contract(): pl.pallas_call(contract_kernel, grid_spec=pltpu.PrefetchScalarGridSpec(nu...]
    dot_general x2 -> x0, matrix products: 6.77 us -> none  [the longest x1 3.64 us: on_device(): jnp.einsum('kij,ir->krj', regrouped, basis_one, precision=lax.Precision.H...]
    ppermute x0 -> x22, waiting for transfers between devices: none -> 4.29 us  [permuted(): return lax.ppermute(value, AXES, pairs)]
    all_to_all x1 -> x0, local copies, waits for them, and re-layouts: 2.9 us -> none  [on_device(): lax.all_to_all(species_field, 'gx', split_axis=0, concat_axis=1, tiled=True)]
  transfers between devices with their start and end apart: 2 -> 24, of which waited for: 2 -> 4; matrix products, arithmetic and copies ran while one was open for 0% -> 7% of each run, Pallas kernels for 0% -> 2%
where the time goes in v1:
time: 127 us
  starting transfers between devices  53.3 us (42%)
  waiting for transfers between devices  47.6 us (37%)
  local copies, waits for them, and re-layouts  15 us (12%)
  Pallas kernels  7.51 us (6%)
  other arithmetic  3.19 us (3%)
    all_to_all x2, waiting for transfers between devices, on_device(): lax.all_to_all(piece, ('y', 'x', 'c'), split_axis=0, concat_axis=0, tiled...  43.3 us
    ppermute x22, starting transfers between devices, permuted(): return lax.ppermute(value, AXES, pairs)  38 us
    all_to_all x2, starting transfers between devices, on_device(): lax.all_to_all(piece, ('y', 'x', 'c'), split_axis=0, concat_axis=0, tiled...  15.3 us
    transpose x3, local copies, waits for them, and re-layouts, on_device(): field[:, :, :, :, start:start + n].transpose(0, 2, 3, 1, 4, 5, 6)  9.09 us
    pallas_call x2, Pallas kernels, contract(): pl.pallas_call(contract_kernel, grid_spec=pltpu.PrefetchScalarGridSpec(nu...  7.51 us
    ppermute x22, waiting for transfers between devices, permuted(): return lax.ppermute(value, AXES, pairs)  4.29 us
    unnamed x14, local copies, waits for them, and re-layouts  2.84 us
  transfers between devices with their start and end apart: 24, of which 4 were waited for; matrix products, arithmetic and copies ran while one was open for 7% of the time, Pallas kernels for 2%

profile of v1, /device:TPU:1, one launch (start us, length us, event | category | flops | bytes accessed | tf_op | source)
XLA Modules:
  0.0 127.0 jit_solution(2708777341278929973)
XLA Ops:
  0.0 4.3 %slice_bitcast_fusion.1 = (f32[4,4,2,2,2,32,128]{6,5,4,2,1,3,0:T(8,128)}, f32[4,4,2,2,2,32,128]{6,5,4,2,1,3,0:T(8,128)S(1)}) fusion(f32[4,2,4,2,4,32,128]{6,5,4,3,2,1,0:T(8,128)} %bitcast.106), kind=kLoop, calls=%fused_computation.1 | loop fusion | bytes 8388608 | tf_op jit(solution)/shard_map/transpose | solution.py:93
  4.3 1.5 %copy.12 = f32[4,4,2,2,2,32,128]{6,5,4,3,2,1,0:T(8,128)} copy(f32[4,4,2,2,2,32,128]{6,5,4,2,1,3,0:T(8,128)S(1)} %get-tuple-element.10) | data formatting | bytes 4194304 | tf_op jit(solution)/shard_map/transpose | solution.py:93
  5.9 8.6 %all-to-all-start.1 = ((f32[128,32,128]{2,1,0:T(8,128)}), f32[128,32,128]{2,1,0:T(8,128)S(1)}, u32[]{:S(2)}, u32[]{:S(2)}) async-start(f32[128,32,128]{2,1,0:T(8,128)} %bitcast.105), calls=%async_computation.1 | async-start | bytes 4194304 | tf_op jit(solution)/shard_map/all_to_all | solution.py:94
  14.5 3.2 %copy.10 = f32[4,4,2,2,2,32,128]{6,5,4,3,2,1,0:T(8,128)} copy(f32[4,4,2,2,2,32,128]{6,5,4,2,1,3,0:T(8,128)} %get-tuple-element.9) | data formatting | bytes 4194304 | tf_op jit(solution)/shard_map/transpose | solution.py:93
  17.7 24.6 %all-to-all-done.1 = f32[128,32,128]{2,1,0:T(8,128)S(1)} async-done(((f32[128,32,128]{2,1,0:T(8,128)}), f32[128,32,128]{2,1,0:T(8,128)S(1)}, u32[]{:S(2)}, u32[]{:S(2)}) %all-to-all-start.1) | async-done | bytes 2097184 | tf_op jit(solution)/shard_map/all_to_all | solution.py:94
  42.3 6.7 %all-to-all-start = ((f32[128,32,128]{2,1,0:T(8,128)}), f32[128,32,128]{2,1,0:T(8,128)}, u32[]{:S(2)}, u32[]{:S(2)}) async-start(f32[128,32,128]{2,1,0:T(8,128)} %bitcast.104), calls=%async_computation | async-start | bytes 4194304 | tf_op jit(solution)/shard_map/all_to_all | solution.py:94
  49.0 0.9 constant_dynamic-slice_fusion.8
  49.9 2.1 %copy.11 = f32[512,256]{0,1:T(8,128)} copy(f32[512,256]{1,0:T(8,128)} %bitcast.107) | data formatting | bytes 1048576 | tf_op jit(solution)/shard_map/reshape | solution.py:88
  52.0 1.0 fusion.1
  53.0 1.2 fusion
  54.1 0.0 copy-start.3
  54.2 3.1 %shard_map.38 = f32[8,2,64,256]{3,2,1,0:T(8,128)S(1)} custom-call(s32[1]{0:T(128)} %bitcast.z_ref, f32[16,2,2,2,32,128]{5,4,3,2,1,0:T(8,128)S(1)} %bitcast.103, bf16[256,512]{1,0:T(8,128)(2,1)S(1)} %get-tuple-element.34.one_h, bf16[256,512]{1,0:T(8,128)(2,1)S(1)} %get-tuple-element.33.one_l, bf16[256,256]{1,0:T(8,128)(2,1)S(1)} %get-tuple-element.32.two_h, ...), custom_call_target="tpu_custom_call" | custom-call | flops 1207959552 | bytes 3145728 | tf_op jit(solution)/shard_map/pallas_call | solution.py:55
  57.3 1.0 copy-done.1
  58.3 18.7 %all-to-all-done = f32[128,32,128]{2,1,0:T(8,128)} async-done(((f32[128,32,128]{2,1,0:T(8,128)}), f32[128,32,128]{2,1,0:T(8,128)}, u32[]{:S(2)}, u32[]{:S(2)}) %all-to-all-start) | async-done | bytes 2097184 | tf_op jit(solution)/shard_map/all_to_all | solution.py:94
  77.0 0.9 copy-done.4
  78.0 0.9 copy-done.6
  78.9 4.4 %shard_map.37 = f32[8,2,64,256]{3,2,1,0:T(8,128)S(1)} custom-call(s32[1]{0:T(128)} %bitcast.z_ref, f32[16,2,2,2,32,128]{5,4,3,2,1,0:T(8,128)} %bitcast.4.x_ref, bf16[256,512]{1,0:T(8,128)(2,1)S(1)} %copy-done.4, bf16[256,512]{1,0:T(8,128)(2,1)S(1)} %get-tuple-element.33.one_l, bf16[256,256]{1,0:T(8,128)(2,1)S(1)} %copy-done.6, ...), custom_call_target="tpu_custom_call" | custom-call | flops 1207959552 | bytes 3145728 | tf_op jit(solution)/shard_map/pallas_call | solution.py:55
  83.3 1.7 %collective-permute-start.11 = (f32[2,32,256]{2,1,0:T(8,128)S(1)}, f32[2,32,256]{2,1,0:T(8,128)S(1)}, u32[]{:S(2)}, u32[]{:S(2)}) collective-permute-start(f32[2,32,256]{2,1,0:T(8,128)S(1)} %get-tuple-element.27), channel_id=1, source_target_pairs={{0,2},{1,3},{8,10},{9,11},{16,18},{17,19},{24,26},{25,27},{2,4},{3... | collective-permute-start | bytes 196616 | tf_op jit(solution)/shard_map/ppermute | solution.py:24
  85.0 4.0 %collective-permute-start.15 = (f32[2,32,256]{2,1,0:T(8,128)S(1)}, f32[2,32,256]{2,1,0:T(8,128)S(1)}, u32[]{:S(2)}, u32[]{:S(2)}) collective-permute-start(f32[2,32,256]{2,1,0:T(8,128)S(1)} %get-tuple-element.28), channel_id=1, source_target_pairs={{0,38},{1,39},{8,46},{9,47},{16,54},{17,55},{24,62},{25,63},{2,0},... | collective-permute-start | bytes 196616 | tf_op jit(solution)/shard_map/ppermute | solution.py:24
  89.1 2.7 %collective-permute-start.19 = (f32[2,32,256]{2,1,0:T(8,128)S(1)}, f32[2,32,256]{2,1,0:T(8,128)S(1)}, u32[]{:S(2)}, u32[]{:S(2)}) collective-permute-start(f32[2,32,256]{2,1,0:T(8,128)S(1)} %dynamic-slice_bitcast_fusion), channel_id=1, source_target_pairs={{0,1},{1,0},{8,9},{9,8},{16,17},{17,16},{24,25},{25,24},{2,3},{3,2... | collective-permute-start | bytes 196616 | tf_op jit(solution)/shard_map/ppermute | solution.py:24
  91.8 0.0 collective-permute-start
  91.8 2.7 %collective-permute-start.4 = (f32[2,32,256]{2,1,0:T(8,128)S(1)}, f32[2,32,256]{2,1,0:T(8,128)S(1)}, u32[]{:S(2)}, u32[]{:S(2)}) collective-permute-start(f32[2,32,256]{2,1,0:T(8,128)S(1)} %get-tuple-element.18), channel_id=1, source_target_pairs={{0,38},{1,39},{8,46},{9,47},{16,54},{17,55},{24,62},{25,63},{2,0},... | collective-permute-start | bytes 196616 | tf_op jit(solution)/shard_map/ppermute | solution.py:24
  94.5 0.0 collective-permute-done.11
  94.5 0.1 collective-permute-start.12
  94.6 2.7 %collective-permute-start.16 = (f32[2,64,256]{2,1,0:T(8,128)S(1)}, f32[2,64,256]{2,1,0:T(8,128)S(1)}, u32[]{:S(2)}, u32[]{:S(2)}) collective-permute-start(f32[2,64,256]{2,1,0:T(8,128)S(1)} %pad_maximum_fusion.3), channel_id=1, source_target_pairs={{0,38},{1,39},{8,46},{9,47},{16,54},{17,55},{24,62},{25,63},{2,0},... | collective-permute-start | bytes 393224 | tf_op jit(solution)/shard_map/ppermute | solution.py:24
  97.4 0.0 collective-permute-done
  97.4 0.0 collective-permute-done.4
  97.4 0.1 collective-permute-start.1
  97.5 2.7 %collective-permute-start.5 = (f32[2,64,256]{2,1,0:T(8,128)S(1)}, f32[2,64,256]{2,1,0:T(8,128)S(1)}, u32[]{:S(2)}, u32[]{:S(2)}) collective-permute-start(f32[2,64,256]{2,1,0:T(8,128)S(1)} %pad_maximum_fusion.1), channel_id=1, source_target_pairs={{0,38},{1,39},{8,46},{9,47},{16,54},{17,55},{24,62},{25,63},{2,0},... | collective-permute-start | bytes 393224 | tf_op jit(solution)/shard_map/ppermute | solution.py:24
  100.3 0.1 collective-permute-start.13
  100.4 2.7 %collective-permute-start.17 = (f32[2,64,256]{2,1,0:T(8,128)S(1)}, f32[2,64,256]{2,1,0:T(8,128)S(1)}, u32[]{:S(2)}, u32[]{:S(2)}) collective-permute-start(f32[2,64,256]{2,1,0:T(8,128)S(1)} %get-tuple-element.24), channel_id=1, source_target_pairs={{0,38},{1,39},{8,46},{9,47},{16,54},{17,55},{24,62},{25,63},{2,0},... | collective-permute-start | bytes 393224 | tf_op jit(solution)/shard_map/ppermute | solution.py:24
  103.1 0.9 collective-permute-start.2
  104.1 2.0 %collective-permute-start.6 = (f32[2,64,256]{2,1,0:T(8,128)S(1)}, f32[2,64,256]{2,1,0:T(8,128)S(1)}, u32[]{:S(2)}, u32[]{:S(2)}) collective-permute-start(f32[2,64,256]{2,1,0:T(8,128)S(1)} %get-tuple-element.14), channel_id=1, source_target_pairs={{0,38},{1,39},{8,46},{9,47},{16,54},{17,55},{24,62},{25,63},{2,0},... | collective-permute-start | bytes 393224 | tf_op jit(solution)/shard_map/ppermute | solution.py:24
  106.1 0.0 collective-permute-done.13
  106.1 0.0 collective-permute-done.17
  106.1 6.2 %collective-permute-start.21 = (f32[2,32,256]{2,1,0:T(8,128)S(1)}, f32[2,32,256]{2,1,0:T(8,128)S(1)}, u32[]{:S(2)}, u32[]{:S(2)}) collective-permute-start(f32[2,32,256]{2,1,0:T(8,128)S(1)} %get-tuple-element.42), channel_id=1, source_target_pairs={{0,39},{1,38},{8,47},{9,46},{16,55},{17,54},{24,63},{25,62},{2,1},... | collective-permute-start | bytes 196616 | tf_op jit(solution)/shard_map/ppermute | solution.py:24
  112.3 0.1 collective-permute-start.20
  112.4 0.0 collective-permute-done.2
  112.4 0.4 collective-permute-start.18
  112.8 0.0 collective-permute-done.6
  112.8 1.1 collective-permute-start.14
  114.0 1.9 %collective-permute-start.8 = (f32[2,32,256]{2,1,0:T(8,128)S(1)}, f32[2,32,256]{2,1,0:T(8,128)S(1)}, u32[]{:S(2)}, u32[]{:S(2)}) collective-permute-start(f32[2,32,256]{2,1,0:T(8,128)S(1)} %dynamic-slice_bitcast_fusion.1), channel_id=1, source_target_pairs={{0,1},{1,0},{8,9},{9,8},{16,17},{17,16},{24,25},{25,24},{2,3},{3,2... | collective-permute-start | bytes 196616 | tf_op jit(solution)/shard_map/ppermute | solution.py:24
  115.9 0.0 collective-permute-done.21
  115.9 2.9 %collective-permute-start.10 = (f32[2,32,256]{2,1,0:T(8,128)S(1)}, f32[2,32,256]{2,1,0:T(8,128)S(1)}, u32[]{:S(2)}, u32[]{:S(2)}) collective-permute-start(f32[2,32,256]{2,1,0:T(8,128)S(1)} %get-tuple-element.38), channel_id=1, source_target_pairs={{0,39},{1,38},{8,47},{9,46},{16,55},{17,54},{24,63},{25,62},{2,1},... | collective-permute-start | bytes 196616 | tf_op jit(solution)/shard_map/ppermute | solution.py:24
  118.9 3.0 %collective-permute-start.7 = (f32[2,32,256]{2,1,0:T(8,128)S(1)}, f32[2,32,256]{2,1,0:T(8,128)S(1)}, u32[]{:S(2)}, u32[]{:S(2)}) collective-permute-start(f32[2,32,256]{2,1,0:T(8,128)S(1)} %get-tuple-element.37), channel_id=1, source_target_pairs={{0,38},{1,39},{8,46},{9,47},{16,54},{17,55},{24,62},{25,63},{2,0},... | collective-permute-start | bytes 196616 | tf_op jit(solution)/shard_map/ppermute | solution.py:24
  122.0 2.3 %collective-permute-done.9 = f32[2,32,256]{2,1,0:T(8,128)S(1)} collective-permute-done((f32[2,32,256]{2,1,0:T(8,128)S(1)}, f32[2,32,256]{2,1,0:T(8,128)S(1)}, u32[]{:S(2)}, u32[]{:S(2)}) %collective-permute-start.9) | collective-permute-done | bytes 65568 | tf_op jit(solution)/shard_map/ppermute | solution.py:24
  124.2 2.0 %collective-permute-done.3 = f32[2,32,256]{2,1,0:T(8,128)S(1)} collective-permute-done((f32[2,32,256]{2,1,0:T(8,128)S(1)}, f32[2,32,256]{2,1,0:T(8,128)S(1)}, u32[]{:S(2)}, u32[]{:S(2)}) %collective-permute-start.3) | collective-permute-done | bytes 65568 | tf_op jit(solution)/shard_map/ppermute | solution.py:24
  126.3 0.7 maximum_maximum_fusion
  (48 shorter events, 0.5 us)
Async XLA Ops:
  0.0 49.0 %copy-start = (f32[1024,256]{1,0:T(8,128)S(1)}, f32[1024,256]{1,0:T(8,128)}, u32[]{:S(2)}) copy-start(f32[1024,256]{1,0:T(8,128)} %param.4) | copy-start | bytes 3145732
  5.9 36.4 %all-to-all-start.1 = ((f32[128,32,128]{2,1,0:T(8,128)}), f32[128,32,128]{2,1,0:T(8,128)S(1)}, u32[]{:S(2)}, u32[]{:S(2)}) async-start(f32[128,32,128]{2,1,0:T(8,128)} %bitcast.105), calls=%async_computation.1 | async-start | bytes 4194304 | tf_op jit(solution)/shard_map/all_to_all | solution.py:94
  42.3 34.7 %all-to-all-start = ((f32[128,32,128]{2,1,0:T(8,128)}), f32[128,32,128]{2,1,0:T(8,128)}, u32[]{:S(2)}, u32[]{:S(2)}) async-start(f32[128,32,128]{2,1,0:T(8,128)} %bitcast.104), calls=%async_computation | async-start | bytes 4194304 | tf_op jit(solution)/shard_map/all_to_all | solution.py:94
  53.0 4.3 %copy-start.5 = (bf16[256,256]{1,0:T(8,128)(2,1)}, bf16[256,256]{1,0:T(8,128)(2,1)S(1)}, u32[]{:S(2)}) copy-start(bf16[256,256]{1,0:T(8,128)(2,1)S(1)} %get-tuple-element.32.two_h) | copy-start | bytes 393220
  54.1 3.1 %copy-start.3 = (bf16[256,512]{1,0:T(8,128)(2,1)}, bf16[256,512]{1,0:T(8,128)(2,1)S(1)}, u32[]{:S(2)}) copy-start(bf16[256,512]{1,0:T(8,128)(2,1)S(1)} %get-tuple-element.34.one_h) | copy-start | bytes 786436
  57.3 1.0 copy-start.1
  77.0 1.0 copy-start.4
  78.0 0.9 copy-start.6
  78.9 15.6 %copy-start.2 = (f32[8,2,64,256]{3,2,1,0:T(8,128)S(1)}, f32[8,2,64,256]{3,2,1,0:T(8,128)}, u32[]{:S(2)}) copy-start(f32[8,2,64,256]{3,2,1,0:T(8,128)} %copy-done.1) | copy-start | bytes 3145732
  83.3 11.1 %collective-permute-start.11 = (f32[2,32,256]{2,1,0:T(8,128)S(1)}, f32[2,32,256]{2,1,0:T(8,128)S(1)}, u32[]{:S(2)}, u32[]{:S(2)}) collective-permute-start(f32[2,32,256]{2,1,0:T(8,128)S(1)} %get-tuple-element.27), channel_id=1, source_target_pairs={{0,2},{1,3},{8,10},{9,11},{16,18},{17,19},{24,26},{25,27},{2,4},{3... | collective-permute-start | bytes 196616 | tf_op jit(solution)/shard_map/ppermute | solution.py:24
  85.0 9.4 %collective-permute-start.15 = (f32[2,32,256]{2,1,0:T(8,128)S(1)}, f32[2,32,256]{2,1,0:T(8,128)S(1)}, u32[]{:S(2)}, u32[]{:S(2)}) collective-permute-start(f32[2,32,256]{2,1,0:T(8,128)S(1)} %get-tuple-element.28), channel_id=1, source_target_pairs={{0,38},{1,39},{8,46},{9,47},{16,54},{17,55},{24,62},{25,63},{2,0},... | collective-permute-start | bytes 196616 | tf_op jit(solution)/shard_map/ppermute | solution.py:24
  89.1 25.0 %collective-permute-start.19 = (f32[2,32,256]{2,1,0:T(8,128)S(1)}, f32[2,32,256]{2,1,0:T(8,128)S(1)}, u32[]{:S(2)}, u32[]{:S(2)}) collective-permute-start(f32[2,32,256]{2,1,0:T(8,128)S(1)} %dynamic-slice_bitcast_fusion), channel_id=1, source_target_pairs={{0,1},{1,0},{8,9},{9,8},{16,17},{17,16},{24,25},{25,24},{2,3},{3,2... | collective-permute-start | bytes 196616 | tf_op jit(solution)/shard_map/ppermute | solution.py:24
  91.8 5.6 %collective-permute-start = (f32[2,32,256]{2,1,0:T(8,128)S(1)}, f32[2,32,256]{2,1,0:T(8,128)S(1)}, u32[]{:S(2)}, u32[]{:S(2)}) collective-permute-start(f32[2,32,256]{2,1,0:T(8,128)S(1)} %get-tuple-element.17), channel_id=1, source_target_pairs={{0,2},{1,3},{8,10},{9,11},{16,18},{17,19},{24,26},{25,27},{2,4},{3... | collective-permute-start | bytes 196616 | tf_op jit(solution)/shard_map/ppermute | solution.py:24
  91.8 5.6 %collective-permute-start.4 = (f32[2,32,256]{2,1,0:T(8,128)S(1)}, f32[2,32,256]{2,1,0:T(8,128)S(1)}, u32[]{:S(2)}, u32[]{:S(2)}) collective-permute-start(f32[2,32,256]{2,1,0:T(8,128)S(1)} %get-tuple-element.18), channel_id=1, source_target_pairs={{0,38},{1,39},{8,46},{9,47},{16,54},{17,55},{24,62},{25,63},{2,0},... | collective-permute-start | bytes 196616 | tf_op jit(solution)/shard_map/ppermute | solution.py:24
  94.5 5.7 %collective-permute-start.12 = (f32[2,64,256]{2,1,0:T(8,128)S(1)}, f32[2,64,256]{2,1,0:T(8,128)S(1)}, u32[]{:S(2)}, u32[]{:S(2)}) collective-permute-start(f32[2,64,256]{2,1,0:T(8,128)S(1)} %pad_maximum_fusion.2), channel_id=1, source_target_pairs={{0,2},{1,3},{8,10},{9,11},{16,18},{17,19},{24,26},{25,27},{2,4},{3... | collective-permute-start | bytes 393224 | tf_op jit(solution)/shard_map/ppermute | solution.py:24
  94.6 5.6 %collective-permute-start.16 = (f32[2,64,256]{2,1,0:T(8,128)S(1)}, f32[2,64,256]{2,1,0:T(8,128)S(1)}, u32[]{:S(2)}, u32[]{:S(2)}) collective-permute-start(f32[2,64,256]{2,1,0:T(8,128)S(1)} %pad_maximum_fusion.3), channel_id=1, source_target_pairs={{0,38},{1,39},{8,46},{9,47},{16,54},{17,55},{24,62},{25,63},{2,0},... | collective-permute-start | bytes 393224 | tf_op jit(solution)/shard_map/ppermute | solution.py:24
  97.4 5.7 %collective-permute-start.1 = (f32[2,64,256]{2,1,0:T(8,128)S(1)}, f32[2,64,256]{2,1,0:T(8,128)S(1)}, u32[]{:S(2)}, u32[]{:S(2)}) collective-permute-start(f32[2,64,256]{2,1,0:T(8,128)S(1)} %pad_maximum_fusion), channel_id=1, source_target_pairs={{0,2},{1,3},{8,10},{9,11},{16,18},{17,19},{24,26},{25,27},{2,4},{3... | collective-permute-start | bytes 393224 | tf_op jit(solution)/shard_map/ppermute | solution.py:24
  97.5 5.5 %collective-permute-start.5 = (f32[2,64,256]{2,1,0:T(8,128)S(1)}, f32[2,64,256]{2,1,0:T(8,128)S(1)}, u32[]{:S(2)}, u32[]{:S(2)}) collective-permute-start(f32[2,64,256]{2,1,0:T(8,128)S(1)} %pad_maximum_fusion.1), channel_id=1, source_target_pairs={{0,38},{1,39},{8,46},{9,47},{16,54},{17,55},{24,62},{25,63},{2,0},... | collective-permute-start | bytes 393224 | tf_op jit(solution)/shard_map/ppermute | solution.py:24
  100.3 5.7 %collective-permute-start.13 = (f32[2,64,256]{2,1,0:T(8,128)S(1)}, f32[2,64,256]{2,1,0:T(8,128)S(1)}, u32[]{:S(2)}, u32[]{:S(2)}) collective-permute-start(f32[2,64,256]{2,1,0:T(8,128)S(1)} %get-tuple-element.23), channel_id=1, source_target_pairs={{0,2},{1,3},{8,10},{9,11},{16,18},{17,19},{24,26},{25,27},{2,4},{3... | collective-permute-start | bytes 393224 | tf_op jit(solution)/shard_map/ppermute | solution.py:24
  100.4 5.7 %collective-permute-start.17 = (f32[2,64,256]{2,1,0:T(8,128)S(1)}, f32[2,64,256]{2,1,0:T(8,128)S(1)}, u32[]{:S(2)}, u32[]{:S(2)}) collective-permute-start(f32[2,64,256]{2,1,0:T(8,128)S(1)} %get-tuple-element.24), channel_id=1, source_target_pairs={{0,38},{1,39},{8,46},{9,47},{16,54},{17,55},{24,62},{25,63},{2,0},... | collective-permute-start | bytes 393224 | tf_op jit(solution)/shard_map/ppermute | solution.py:24
  103.1 9.3 %collective-permute-start.2 = (f32[2,64,256]{2,1,0:T(8,128)S(1)}, f32[2,64,256]{2,1,0:T(8,128)S(1)}, u32[]{:S(2)}, u32[]{:S(2)}) collective-permute-start(f32[2,64,256]{2,1,0:T(8,128)S(1)} %get-tuple-element.13), channel_id=1, source_target_pairs={{0,2},{1,3},{8,10},{9,11},{16,18},{17,19},{24,26},{25,27},{2,4},{3... | collective-permute-start | bytes 393224 | tf_op jit(solution)/shard_map/ppermute | solution.py:24
  104.1 8.8 %collective-permute-start.6 = (f32[2,64,256]{2,1,0:T(8,128)S(1)}, f32[2,64,256]{2,1,0:T(8,128)S(1)}, u32[]{:S(2)}, u32[]{:S(2)}) collective-permute-start(f32[2,64,256]{2,1,0:T(8,128)S(1)} %get-tuple-element.14), channel_id=1, source_target_pairs={{0,38},{1,39},{8,46},{9,47},{16,54},{17,55},{24,62},{25,63},{2,0},... | collective-permute-start | bytes 393224 | tf_op jit(solution)/shard_map/ppermute | solution.py:24
  106.1 9.8 %collective-permute-start.21 = (f32[2,32,256]{2,1,0:T(8,128)S(1)}, f32[2,32,256]{2,1,0:T(8,128)S(1)}, u32[]{:S(2)}, u32[]{:S(2)}) collective-permute-start(f32[2,32,256]{2,1,0:T(8,128)S(1)} %get-tuple-element.42), channel_id=1, source_target_pairs={{0,39},{1,38},{8,47},{9,46},{16,55},{17,54},{24,63},{25,62},{2,1},... | collective-permute-start | bytes 196616 | tf_op jit(solution)/shard_map/ppermute | solution.py:24
  112.3 6.6 %collective-permute-start.20 = (f32[2,32,256]{2,1,0:T(8,128)S(1)}, f32[2,32,256]{2,1,0:T(8,128)S(1)}, u32[]{:S(2)}, u32[]{:S(2)}) collective-permute-start(f32[2,32,256]{2,1,0:T(8,128)S(1)} %get-tuple-element.40), channel_id=1, source_target_pairs={{0,3},{1,2},{8,11},{9,10},{16,19},{17,18},{24,27},{25,26},{2,5},{3... | collective-permute-start | bytes 196616 | tf_op jit(solution)/shard_map/ppermute | solution.py:24
  112.4 6.5 %collective-permute-start.18 = (f32[2,32,256]{2,1,0:T(8,128)S(1)}, f32[2,32,256]{2,1,0:T(8,128)S(1)}, u32[]{:S(2)}, u32[]{:S(2)}) collective-permute-start(f32[2,32,256]{2,1,0:T(8,128)S(1)} %get-tuple-element.41), channel_id=1, source_target_pairs={{0,38},{1,39},{8,46},{9,47},{16,54},{17,55},{24,62},{25,63},{2,0},... | collective-permute-start | bytes 196616 | tf_op jit(solution)/shard_map/ppermute | solution.py:24
  112.8 9.1 %collective-permute-start.14 = (f32[2,32,256]{2,1,0:T(8,128)S(1)}, f32[2,32,256]{2,1,0:T(8,128)S(1)}, u32[]{:S(2)}, u32[]{:S(2)}) collective-permute-start(f32[2,32,256]{2,1,0:T(8,128)S(1)} %get-tuple-element.39), channel_id=1, source_target_pairs={{0,2},{1,3},{8,10},{9,11},{16,18},{17,19},{24,26},{25,27},{2,4},{3... | collective-permute-start | bytes 196616 | tf_op jit(solution)/shard_map/ppermute | solution.py:24
  114.0 7.9 %collective-permute-start.8 = (f32[2,32,256]{2,1,0:T(8,128)S(1)}, f32[2,32,256]{2,1,0:T(8,128)S(1)}, u32[]{:S(2)}, u32[]{:S(2)}) collective-permute-start(f32[2,32,256]{2,1,0:T(8,128)S(1)} %dynamic-slice_bitcast_fusion.1), channel_id=1, source_target_pairs={{0,1},{1,0},{8,9},{9,8},{16,17},{17,16},{24,25},{25,24},{2,3},{3,2... | collective-permute-start | bytes 196616 | tf_op jit(solution)/shard_map/ppermute | solution.py:24
  115.9 6.0 %collective-permute-start.10 = (f32[2,32,256]{2,1,0:T(8,128)S(1)}, f32[2,32,256]{2,1,0:T(8,128)S(1)}, u32[]{:S(2)}, u32[]{:S(2)}) collective-permute-start(f32[2,32,256]{2,1,0:T(8,128)S(1)} %get-tuple-element.38), channel_id=1, source_target_pairs={{0,39},{1,38},{8,47},{9,46},{16,55},{17,54},{24,63},{25,62},{2,1},... | collective-permute-start | bytes 196616 | tf_op jit(solution)/shard_map/ppermute | solution.py:24
  118.9 5.4 %collective-permute-start.9 = (f32[2,32,256]{2,1,0:T(8,128)S(1)}, f32[2,32,256]{2,1,0:T(8,128)S(1)}, u32[]{:S(2)}, u32[]{:S(2)}) collective-permute-start(f32[2,32,256]{2,1,0:T(8,128)S(1)} %get-tuple-element.36), channel_id=1, source_target_pairs={{0,3},{1,2},{8,11},{9,10},{16,19},{17,18},{24,27},{25,26},{2,5},{3... | collective-permute-start | bytes 196616 | tf_op jit(solution)/shard_map/ppermute | solution.py:24
  118.9 5.4 %collective-permute-start.7 = (f32[2,32,256]{2,1,0:T(8,128)S(1)}, f32[2,32,256]{2,1,0:T(8,128)S(1)}, u32[]{:S(2)}, u32[]{:S(2)}) collective-permute-start(f32[2,32,256]{2,1,0:T(8,128)S(1)} %get-tuple-element.37), channel_id=1, source_target_pairs={{0,38},{1,39},{8,46},{9,47},{16,54},{17,55},{24,62},{25,63},{2,0},... | collective-permute-start | bytes 196616 | tf_op jit(solution)/shard_map/ppermute | solution.py:24
  121.9 4.3 %collective-permute-start.3 = (f32[2,32,256]{2,1,0:T(8,128)S(1)}, f32[2,32,256]{2,1,0:T(8,128)S(1)}, u32[]{:S(2)}, u32[]{:S(2)}) collective-permute-start(f32[2,32,256]{2,1,0:T(8,128)S(1)} %get-tuple-element.35), channel_id=1, source_target_pairs={{0,2},{1,3},{8,10},{9,11},{16,18},{17,19},{24,26},{25,27},{2,4},{3... | collective-permute-start | bytes 196616 | tf_op jit(solution)/shard_map/ppermute | solution.py:24

commit v2 on v0

v2 whole, which is shorter than its diff:
```python
import functools

import jax
import jax.numpy as jnp
from jax import lax
from jax.experimental import pallas as pl
from jax.experimental.pallas import tpu as pltpu
from jax.sharding import Mesh, PartitionSpec as P

AXES = ("y", "zh", "x", "zl", "c")
SIZES = (4, 2, 4, 4, 2)
PLANE = ("y", "x", "c")
VMEM = pl.BlockSpec(memory_space=pltpu.VMEM)
SMEM = pl.BlockSpec(memory_space=pltpu.SMEM)
ANY = pl.BlockSpec(memory_space=pl.ANY)
f32 = functools.partial(jax.ShapeDtypeStruct, dtype=jnp.float32)
dot = functools.partial(jnp.dot, preferred_element_type=jnp.float32)
params = functools.partial(pltpu.CompilerParams, vmem_limit_bytes=20 << 20)


def along(value, dz, flip=0):
    pairs = []
    for y in range(4):
        for z in range(8):
            for x in range(4):
                for c in range(2):

                    def at(z, c):
                        return (((y * 2 + z // 4) * 4 + x) * 4 + z % 4) * 2 + c

                    pairs.append((at(z, c), at((z + dz) % 8, c ^ flip)))
    return lax.ppermute(value, AXES, pairs)


def split(value):
    high = value.astype(jnp.bfloat16)
    return high, (value - high.astype(jnp.float32)).astype(jnp.bfloat16)


def pack_kernel(field_ref, packed_ref, sems):
    copies = []
    for zh in range(2):
        for c in range(2):
            copies.append(pltpu.make_async_copy(field_ref.at[:, zh, :, c], packed_ref.at[:, :, c, zh], sems.at[2 * zh + c]))
    for copy in copies:
        copy.start()
    for copy in copies:
        copy.wait()


def pack(field):
    return pl.pallas_call(
        pack_kernel,
        in_specs=[ANY],
        out_specs=VMEM,
        out_shape=f32((4, 4, 2, 2, 4, 32, 128)),
        scratch_shapes=[pltpu.SemaphoreType.DMA((4,))],
        compiler_params=params(),
    )(field)


def prepare_kernel(one_ref, two_ref, one_out, two_out):
    for zh in range(2):
        high, low = split(one_ref[:, zh].reshape(512, 256).T)
        one_out[zh] = jnp.concatenate([high, high, low], axis=1)
    for zl in range(4):
        high, low = split(two_ref[256 * zl:256 * zl + 256])
        two_out[zl] = jnp.concatenate([high, high, low], axis=0)


def prepare(basis_one, basis_two):
    return pl.pallas_call(
        prepare_kernel,
        in_specs=[VMEM] * 2,
        out_specs=[VMEM] * 2,
        out_shape=[jax.ShapeDtypeStruct((2, 256, 1536), jnp.bfloat16), jax.ShapeDtypeStruct((4, 768, 256), jnp.bfloat16)],
        compiler_params=params(),
        cost_estimate=pl.CostEstimate(flops=1 << 26, bytes_accessed=5 << 20, transcendentals=0),
    )(basis_one.reshape(4, 2, 4, 32, 256), basis_two)


def first_kernel(at_ref, x_ref, one_ref, two_ref, out_ref, reduced_ref):
    z, core = at_ref[0], at_ref[1]
    one, two = one_ref[z // 4], two_ref[z % 4]
    for t in range(8):
        block = jnp.concatenate([x_ref[:, c, t // 4, t % 4].reshape(512, 128) for c in range(2)], axis=1)
        high, low = split(block)
        high, low = split(dot(one, jnp.concatenate([high, low, high], axis=0)))
        reduced_ref[t] = jnp.concatenate([high, low, high], axis=1)
    partial = dot(reduced_ref[...].reshape(2048, 768), two).reshape(8, 256, 256)
    for t in range(8):
        for b in range(8):
            away = (t // 4 * 4 + b // 2 + 8 - z) % 8
            out_ref[away, (b % 2) ^ core, t % 4] = partial[t, 32 * b:32 * b + 32]


def first_contract(at, received, one, two):
    return pl.pallas_call(
        first_kernel,
        in_specs=[SMEM, VMEM, VMEM, VMEM],
        out_specs=VMEM,
        out_shape=f32((8, 2, 4, 32, 256)),
        scratch_shapes=[pltpu.VMEM((8, 256, 768), jnp.bfloat16)],
        compiler_params=params(),
        cost_estimate=pl.CostEstimate(flops=8 * 3 * 2 * 256 * 256 * 768, bytes_accessed=6 << 20, transcendentals=0),
    )(at, received, one, two)


def finish_kernel(at_ref, first_ref, up_ref, down_ref, swapped_ref, up_cross_ref, down_cross_ref, out_ref):
    core = at_ref[1]
    out_ref[pl.ds(4 * core, 4)] = first_ref[...] + (up_ref[...] + down_ref[...])
    out_ref[pl.ds(4 - 4 * core, 4)] = swapped_ref[...] + (up_cross_ref[...] + down_cross_ref[...])


def finish(at, *pieces):
    return pl.pallas_call(
        finish_kernel,
        in_specs=[SMEM] + [VMEM] * 6,
        out_specs=VMEM,
        out_shape=f32((8, 32, 256)),
        compiler_params=params(),
    )(at, *pieces)


def on_device(species_field, basis_one, basis_two):
    zh, zl, c = lax.axis_index("zh"), lax.axis_index("zl"), lax.axis_index("c")
    z = zh * 4 + zl
    at = jnp.stack([z, c]).astype(jnp.int32)
    packed = pack(species_field.reshape(4, 2, 4, 2, 4, 32, 128)).reshape(256, 32, 128)
    packed, at, one, two = lax.optimization_barrier((packed, at, *prepare(basis_one, basis_two)))
    moved = lax.all_to_all(packed, PLANE, split_axis=0, concat_axis=0, tiled=True)
    parts = first_contract(at, moved.reshape(16, 2, 2, 4, 32, 128), one, two)
    up, down = along(parts[4, 0], 1), along(parts[4, 1], -1)
    swapped = along(parts[0, 1], 0, 1)
    up = jnp.stack([parts[3, 0] + up, parts[3, 1]])
    down = jnp.stack([parts[5, 0], parts[5, 1] + down])
    up, down = along(up, 1) + parts[2], along(down, -1) + parts[6]
    up, down = along(up, 1) + parts[1], along(down, -1) + parts[7]
    ends = [along(up[0], 1), along(down[0], -1), swapped, along(up[1], 1, 1), along(down[1], -1, 1)]

    return finish(at, parts[0, 0], *ends)


def solution(mesh):
    fine = Mesh(mesh.devices.reshape(SIZES), AXES)
    placed = (P(None, ("y", "zh", "x"), ("zl", "c")), P(), P())
    return jax.shard_map(
        on_device, mesh=fine, in_specs=placed, out_specs=P(("y", "zh", "x"), ("zl", "c"), None), check_vma=False
    )
```

time: 175 us -> 111 us (0.63); the launches traced: 173 us -> 111 us
  waiting for transfers between devices: 135 us -> 21.3 us
  blocking collectives: 0 us -> 59.5 us
  between operations: 13.4 us -> 0.1 us
  matrix products: 6.77 us -> 0 us
  Pallas kernels: 0 us -> 5.52 us
  starting transfers between devices: 14.8 us -> 20.1 us
    all_to_all x1 -> x0, waiting for transfers between devices: 69.8 us -> none  [on_device(): lax.all_to_all(species_field, 'gx', split_axis=0, concat_axis=1, tiled=True)]
    reduce_scatter x1 -> x0, waiting for transfers between devices: 65.5 us -> none  [on_device(): lax.psum_scatter(partial_core, 'gy', scatter_dimension=1, tiled=True)]
    all_to_all x0 -> x1, blocking collectives: none -> 59.5 us  [on_device(): lax.all_to_all(packed, PLANE, split_axis=0, concat_axis=0, tiled=True)]
    ppermute x0 -> x11, waiting for transfers between devices: none -> 21.3 us  [along(): return lax.ppermute(value, AXES, pairs)]
    ppermute x0 -> x11, starting transfers between devices: none -> 20.1 us  [along(): return lax.ppermute(value, AXES, pairs)]
    all_to_all x1 -> x0, starting transfers between devices: 14.8 us -> none  [on_device(): lax.all_to_all(species_field, 'gx', split_axis=0, concat_axis=1, tiled=True)]
    dot_general x2 -> x0, matrix products: 6.77 us -> none  [the longest x1 3.64 us: on_device(): jnp.einsum('kij,ir->krj', regrouped, basis_one, precision=lax.Precision.H...]
    pallas_call x0 -> x4, Pallas kernels: none -> 5.52 us  [the longest x1 3.36 us: first_contract(): pl.pallas_call(first_kernel, in_specs=[SMEM, VMEM, VMEM, VMEM], out_specs...]
  transfers between devices with their start and end apart: 2 -> 11, of which waited for: 2 -> 9; matrix products, arithmetic and copies ran while one was open for 0% -> 0% of each run, Pallas kernels for 0% -> 0%
where the time goes in v2:
time: 111 us
  blocking collectives  59.5 us (54%)
  waiting for transfers between devices  21.3 us (19%)
  starting transfers between devices  20.1 us (18%)
  Pallas kernels  5.52 us (5%)
  local copies, waits for them, and re-layouts  4.22 us (4%)
    all_to_all x1, blocking collectives, on_device(): lax.all_to_all(packed, PLANE, split_axis=0, concat_axis=0, tiled=True)  59.5 us
    ppermute x11, waiting for transfers between devices, along(): return lax.ppermute(value, AXES, pairs)  21.3 us
    ppermute x11, starting transfers between devices, along(): return lax.ppermute(value, AXES, pairs)  20.1 us
    unnamed x8, local copies, waits for them, and re-layouts  4.13 us
    pallas_call x1, Pallas kernels, first_contract(): pl.pallas_call(first_kernel, in_specs=[SMEM, VMEM, VMEM, VMEM], out_specs...  3.36 us
  transfers between devices with their start and end apart: 11, of which 9 were waited for; matrix products, arithmetic and copies ran while one was open for 0% of the time, Pallas kernels for 0%

profile of v2, /device:TPU:1, one launch (start us, length us, event | category | flops | bytes accessed | tf_op | source)
XLA Modules:
  0.0 111.0 jit_solution(15696558135046392772)
XLA Ops:
  0.0 0.0 copy-start.1
  0.0 2.2 %copy-done.1 = f32[256,32,128]{2,1,0:T(8,128)S(1)} copy-done((f32[256,32,128]{2,1,0:T(8,128)S(1)}, f32[256,32,128]{2,1,0:T(8,128)}, u32[]{:S(2)}) %copy-start.1) | copy-done | bytes 4194328
  2.2 0.0 copy-start.2
  2.2 0.0 copy-start.3
  2.2 0.3 shard_map.37
  2.5 0.0 copy-start
  2.5 1.9 %copy-done = f32[4,4,2,2,4,32,128]{6,5,4,3,2,1,0:T(8,128)} copy-done((f32[4,4,2,2,4,32,128]{6,5,4,3,2,1,0:T(8,128)}, f32[4,4,2,2,4,32,128]{6,5,4,3,2,1,0:T(8,128)S(1)}, u32[]{:S(2)}) %copy-start) | copy-done | bytes 4194328
  4.5 0.1 pad_add_fusion.at_ref
  4.5 0.0 copy-done.2
  4.5 0.0 copy-done.3
  4.5 0.6 shard_map.38
  5.1 59.5 %all_to_all.5 = f32[256,32,128]{2,1,0:T(8,128)S(1)} all-to-all(f32[256,32,128]{2,1,0:T(8,128)} %bitcast.59), channel_id=1, replica_groups=mesh['y'=4,'zh'=2,'x'=4,'zl'=4,'c'=2] {'y','x','c'}, dimensions={0} | all-to-all | bytes 8388608 | tf_op jit(solution)/shard_map/all_to_all | solution.py:131
  64.6 3.4 %shard_map.39 = f32[8,2,4,32,256]{4,3,2,1,0:T(8,128)S(1)} custom-call(s32[2]{0:T(128)S(1)} %pad_add_fusion.at_ref, f32[16,2,2,4,32,128]{5,4,3,2,1,0:T(8,128)S(1)} %bitcast.58, bf16[2,256,1536]{2,1,0:T(8,128)(2,1)S(1)} %get-tuple-element.15.one_ref, bf16[4,768,256]{2,1,0:T(8,128)(2,1)S(1)} %get-tuple-element.16.two_ref), custom_call_target="tpu_custom_call" | custom-call | flops 2415919104 | bytes 6291456 | tf_op jit(solution)/shard_map/pallas_call | solution.py:98
  68.0 0.1 slice_bitcast_fusion.6
  68.0 5.7 %collective-permute-start.4 = (f32[4,32,256]{2,1,0:T(8,128)S(1)}, f32[4,32,256]{2,1,0:T(8,128)S(1)}, u32[]{:S(2)}, u32[]{:S(2)}) collective-permute-start(f32[4,32,256]{2,1,0:T(8,128)S(1)} %get-tuple-element.18), channel_id=1, source_target_pairs={{0,38},{1,39},{8,46},{9,47},{16,54},{17,55},{24,62},{25,63},{2,0},... | collective-permute-start | bytes 393224 | tf_op jit(solution)/shard_map/ppermute | solution.py:32
  73.7 0.0 collective-permute-start
  73.7 2.5 %collective-permute-done.4 = f32[4,32,256]{2,1,0:T(8,128)S(1)} collective-permute-done((f32[4,32,256]{2,1,0:T(8,128)S(1)}, f32[4,32,256]{2,1,0:T(8,128)S(1)}, u32[]{:S(2)}, u32[]{:S(2)}) %collective-permute-start.4) | collective-permute-done | bytes 131104 | tf_op jit(solution)/shard_map/ppermute | solution.py:32
  76.2 3.1 %collective-permute-done = f32[4,32,256]{2,1,0:T(8,128)S(1)} collective-permute-done((f32[4,32,256]{2,1,0:T(8,128)S(1)}, f32[4,32,256]{2,1,0:T(8,128)S(1)}, u32[]{:S(2)}, u32[]{:S(2)}) %collective-permute-start) | collective-permute-done | bytes 131104 | tf_op jit(solution)/shard_map/ppermute | solution.py:32
  79.3 0.1 collective-permute-start.1
  79.4 2.7 %collective-permute-start.5 = (f32[2,4,32,256]{3,2,1,0:T(8,128)S(1)}, f32[2,4,32,256]{3,2,1,0:T(8,128)S(1)}, u32[]{:S(2)}, u32[]{:S(2)}) collective-permute-start(f32[2,4,32,256]{3,2,1,0:T(8,128)S(1)} %pad_maximum_fusion.1), channel_id=1, source_target_pairs={{0,38},{1,39},{8,46},{9,47},{16,54},{17,55},{24,62},{25,63},{2,0},... | collective-permute-start | bytes 786440 | tf_op jit(solution)/shard_map/ppermute | solution.py:32
  82.2 4.7 %collective-permute-done.1 = f32[2,4,32,256]{3,2,1,0:T(8,128)S(1)} collective-permute-done((f32[2,4,32,256]{3,2,1,0:T(8,128)S(1)}, f32[2,4,32,256]{3,2,1,0:T(8,128)S(1)}, u32[]{:S(2)}, u32[]{:S(2)}) %collective-permute-start.1) | collective-permute-done | bytes 262176 | tf_op jit(solution)/shard_map/ppermute | solution.py:32
  86.9 0.0 collective-permute-done.5
  86.9 0.1 fusion.1
  86.9 2.6 %collective-permute-start.6 = (f32[2,4,32,256]{3,2,1,0:T(8,128)S(1)}, f32[2,4,32,256]{3,2,1,0:T(8,128)S(1)}, u32[]{:S(2)}, u32[]{:S(2)}) collective-permute-start(f32[2,4,32,256]{3,2,1,0:T(8,128)S(1)} %get-tuple-element.25), channel_id=1, source_target_pairs={{0,38},{1,39},{8,46},{9,47},{16,54},{17,55},{24,62},{25,63},{2,0},... | collective-permute-start | bytes 786440 | tf_op jit(solution)/shard_map/ppermute | solution.py:32
  89.5 0.0 collective-permute-start.2
  89.5 3.0 %collective-permute-start.8 = (f32[4,32,256]{2,1,0:T(8,128)S(1)}, f32[4,32,256]{2,1,0:T(8,128)S(1)}, u32[]{:S(2)}, u32[]{:S(2)}) collective-permute-start(f32[4,32,256]{2,1,0:T(8,128)S(1)} %get-tuple-element.17), channel_id=1, source_target_pairs={{0,1},{1,0},{8,9},{9,8},{16,17},{17,16},{24,25},{25,24},{2,3},{3,2... | collective-permute-start | bytes 393224 | tf_op jit(solution)/shard_map/ppermute | solution.py:32
  92.5 0.3 collective-permute-done.6
  92.8 3.1 %collective-permute-done.2 = f32[2,4,32,256]{3,2,1,0:T(8,128)S(1)} collective-permute-done((f32[2,4,32,256]{3,2,1,0:T(8,128)S(1)}, f32[2,4,32,256]{3,2,1,0:T(8,128)S(1)}, u32[]{:S(2)}, u32[]{:S(2)}) %collective-permute-start.2) | collective-permute-done | bytes 262176 | tf_op jit(solution)/shard_map/ppermute | solution.py:32
  95.9 0.1 fusion
  96.0 3.9 %collective-permute-start.10 = (f32[4,32,256]{2,1,0:T(8,128)S(1)}, f32[4,32,256]{2,1,0:T(8,128)S(1)}, u32[]{:S(2)}, u32[]{:S(2)}) collective-permute-start(f32[4,32,256]{2,1,0:T(8,128)S(1)} %get-tuple-element.29), channel_id=1, source_target_pairs={{0,39},{1,38},{8,47},{9,46},{16,55},{17,54},{24,63},{25,62},{2,1},... | collective-permute-start | bytes 393224 | tf_op jit(solution)/shard_map/ppermute | solution.py:32
  99.9 0.0 collective-permute-start.7
  99.9 2.2 %collective-permute-start.9 = (f32[4,32,256]{2,1,0:T(8,128)S(1)}, f32[4,32,256]{2,1,0:T(8,128)S(1)}, u32[]{:S(2)}, u32[]{:S(2)}) collective-permute-start(f32[4,32,256]{2,1,0:T(8,128)S(1)} %get-tuple-element.31), channel_id=1, source_target_pairs={{0,3},{1,2},{8,11},{9,10},{16,19},{17,18},{24,27},{25,26},{2,5},{3... | collective-permute-start | bytes 393224 | tf_op jit(solution)/shard_map/ppermute | solution.py:32
  102.1 0.0 collective-permute-start.3
  102.1 0.0 collective-permute-done.8.swapped_ref
  102.1 0.6 collective-permute-done.10.down_cross_ref
  102.7 4.2 %collective-permute-done.7.down_ref = f32[4,32,256]{2,1,0:T(8,128)S(1)} collective-permute-done((f32[4,32,256]{2,1,0:T(8,128)S(1)}, f32[4,32,256]{2,1,0:T(8,128)S(1)}, u32[]{:S(2)}, u32[]{:S(2)}) %collective-permute-start.7) | collective-permute-done | bytes 131104 | tf_op jit(solution)/shard_map/ppermute | solution.py:32
  106.9 0.1 collective-permute-done.9.up_cross_ref
  107.0 2.7 %collective-permute-done.3.up_ref = f32[4,32,256]{2,1,0:T(8,128)S(1)} collective-permute-done((f32[4,32,256]{2,1,0:T(8,128)S(1)}, f32[4,32,256]{2,1,0:T(8,128)S(1)}, u32[]{:S(2)}, u32[]{:S(2)}) %collective-permute-start.3) | collective-permute-done | bytes 131104 | tf_op jit(solution)/shard_map/ppermute | solution.py:32
  109.7 1.3 %shard_map.40 = f32[8,32,256]{2,1,0:T(8,128)} custom-call(s32[2]{0:T(128)S(1)} %pad_add_fusion.at_ref, f32[4,32,256]{2,1,0:T(8,128)S(1)} %get-tuple-element.22.first_ref, f32[4,32,256]{2,1,0:T(8,128)S(1)} %collective-permute-done.3.up_ref, f32[4,32,256]{2,1,0:T(8,128)S(1)} %collective-permute-done.7.down_ref, ...), custom_call_target="tpu_custom_call" | custom-call | tf_op jit(solution)/shard_map/pallas_call | solution.py:116
  (5 shorter events, 0.1 us)
Async XLA Ops:
  0.0 2.2 %copy-start.1 = (f32[256,32,128]{2,1,0:T(8,128)S(1)}, f32[256,32,128]{2,1,0:T(8,128)}, u32[]{:S(2)}) copy-start(f32[256,32,128]{2,1,0:T(8,128)} %param.3) | copy-start | bytes 12582916
  2.2 2.4 %copy-start.2 = (f32[1024,256]{1,0:T(8,128)S(1)}, f32[1024,256]{1,0:T(8,128)}, u32[]{:S(2)}) copy-start(f32[1024,256]{1,0:T(8,128)} %param.4) | copy-start | bytes 3145732
  2.2 2.4 %copy-start.3 = (f32[1024,256]{1,0:T(8,128)S(1)}, f32[1024,256]{1,0:T(8,128)}, u32[]{:S(2)}) copy-start(f32[1024,256]{1,0:T(8,128)} %two_ref.1) | copy-start | bytes 3145732
  2.5 1.9 %copy-start = (f32[4,4,2,2,4,32,128]{6,5,4,3,2,1,0:T(8,128)}, f32[4,4,2,2,4,32,128]{6,5,4,3,2,1,0:T(8,128)S(1)}, u32[]{:S(2)}) copy-start(f32[4,4,2,2,4,32,128]{6,5,4,3,2,1,0:T(8,128)S(1)} %shard_map.37) | copy-start | bytes 12582916
  68.0 8.1 %collective-permute-start.4 = (f32[4,32,256]{2,1,0:T(8,128)S(1)}, f32[4,32,256]{2,1,0:T(8,128)S(1)}, u32[]{:S(2)}, u32[]{:S(2)}) collective-permute-start(f32[4,32,256]{2,1,0:T(8,128)S(1)} %get-tuple-element.18), channel_id=1, source_target_pairs={{0,38},{1,39},{8,46},{9,47},{16,54},{17,55},{24,62},{25,63},{2,0},... | collective-permute-start | bytes 393224 | tf_op jit(solution)/shard_map/ppermute | solution.py:32
  73.7 5.6 %collective-permute-start = (f32[4,32,256]{2,1,0:T(8,128)S(1)}, f32[4,32,256]{2,1,0:T(8,128)S(1)}, u32[]{:S(2)}, u32[]{:S(2)}) collective-permute-start(f32[4,32,256]{2,1,0:T(8,128)S(1)} %get-tuple-element.21), channel_id=1, source_target_pairs={{0,2},{1,3},{8,10},{9,11},{16,18},{17,19},{24,26},{25,27},{2,4},{3... | collective-permute-start | bytes 393224 | tf_op jit(solution)/shard_map/ppermute | solution.py:32
  79.3 7.5 %collective-permute-start.1 = (f32[2,4,32,256]{3,2,1,0:T(8,128)S(1)}, f32[2,4,32,256]{3,2,1,0:T(8,128)S(1)}, u32[]{:S(2)}, u32[]{:S(2)}) collective-permute-start(f32[2,4,32,256]{3,2,1,0:T(8,128)S(1)} %pad_maximum_fusion), channel_id=1, source_target_pairs={{0,2},{1,3},{8,10},{9,11},{16,18},{17,19},{24,26},{25,27},{2,4},{3... | collective-permute-start | bytes 786440 | tf_op jit(solution)/shard_map/ppermute | solution.py:32
  79.4 7.4 %collective-permute-start.5 = (f32[2,4,32,256]{3,2,1,0:T(8,128)S(1)}, f32[2,4,32,256]{3,2,1,0:T(8,128)S(1)}, u32[]{:S(2)}, u32[]{:S(2)}) collective-permute-start(f32[2,4,32,256]{3,2,1,0:T(8,128)S(1)} %pad_maximum_fusion.1), channel_id=1, source_target_pairs={{0,38},{1,39},{8,46},{9,47},{16,54},{17,55},{24,62},{25,63},{2,0},... | collective-permute-start | bytes 786440 | tf_op jit(solution)/shard_map/ppermute | solution.py:32
  86.9 5.9 %collective-permute-start.6 = (f32[2,4,32,256]{3,2,1,0:T(8,128)S(1)}, f32[2,4,32,256]{3,2,1,0:T(8,128)S(1)}, u32[]{:S(2)}, u32[]{:S(2)}) collective-permute-start(f32[2,4,32,256]{3,2,1,0:T(8,128)S(1)} %get-tuple-element.25), channel_id=1, source_target_pairs={{0,38},{1,39},{8,46},{9,47},{16,54},{17,55},{24,62},{25,63},{2,0},... | collective-permute-start | bytes 786440 | tf_op jit(solution)/shard_map/ppermute | solution.py:32
  89.5 6.4 %collective-permute-start.2 = (f32[2,4,32,256]{3,2,1,0:T(8,128)S(1)}, f32[2,4,32,256]{3,2,1,0:T(8,128)S(1)}, u32[]{:S(2)}, u32[]{:S(2)}) collective-permute-start(f32[2,4,32,256]{3,2,1,0:T(8,128)S(1)} %get-tuple-element.26), channel_id=1, source_target_pairs={{0,2},{1,3},{8,10},{9,11},{16,18},{17,19},{24,26},{25,27},{2,4},{3... | collective-permute-start | bytes 786440 | tf_op jit(solution)/shard_map/ppermute | solution.py:32
  89.5 12.6 %collective-permute-start.8 = (f32[4,32,256]{2,1,0:T(8,128)S(1)}, f32[4,32,256]{2,1,0:T(8,128)S(1)}, u32[]{:S(2)}, u32[]{:S(2)}) collective-permute-start(f32[4,32,256]{2,1,0:T(8,128)S(1)} %get-tuple-element.17), channel_id=1, source_target_pairs={{0,1},{1,0},{8,9},{9,8},{16,17},{17,16},{24,25},{25,24},{2,3},{3,2... | collective-permute-start | bytes 393224 | tf_op jit(solution)/shard_map/ppermute | solution.py:32
  96.0 6.7 %collective-permute-start.10 = (f32[4,32,256]{2,1,0:T(8,128)S(1)}, f32[4,32,256]{2,1,0:T(8,128)S(1)}, u32[]{:S(2)}, u32[]{:S(2)}) collective-permute-start(f32[4,32,256]{2,1,0:T(8,128)S(1)} %get-tuple-element.29), channel_id=1, source_target_pairs={{0,39},{1,38},{8,47},{9,46},{16,55},{17,54},{24,63},{25,62},{2,1},... | collective-permute-start | bytes 393224 | tf_op jit(solution)/shard_map/ppermute | solution.py:32
  99.9 7.0 %collective-permute-start.7 = (f32[4,32,256]{2,1,0:T(8,128)S(1)}, f32[4,32,256]{2,1,0:T(8,128)S(1)}, u32[]{:S(2)}, u32[]{:S(2)}) collective-permute-start(f32[4,32,256]{2,1,0:T(8,128)S(1)} %get-tuple-element.30), channel_id=1, source_target_pairs={{0,38},{1,39},{8,46},{9,47},{16,54},{17,55},{24,62},{25,63},{2,0},... | collective-permute-start | bytes 393224 | tf_op jit(solution)/shard_map/ppermute | solution.py:32
  99.9 7.1 %collective-permute-start.9 = (f32[4,32,256]{2,1,0:T(8,128)S(1)}, f32[4,32,256]{2,1,0:T(8,128)S(1)}, u32[]{:S(2)}, u32[]{:S(2)}) collective-permute-start(f32[4,32,256]{2,1,0:T(8,128)S(1)} %get-tuple-element.31), channel_id=1, source_target_pairs={{0,3},{1,2},{8,11},{9,10},{16,19},{17,18},{24,27},{25,26},{2,5},{3... | collective-permute-start | bytes 393224 | tf_op jit(solution)/shard_map/ppermute | solution.py:32
  102.1 7.6 %collective-permute-start.3 = (f32[4,32,256]{2,1,0:T(8,128)S(1)}, f32[4,32,256]{2,1,0:T(8,128)S(1)}, u32[]{:S(2)}, u32[]{:S(2)}) collective-permute-start(f32[4,32,256]{2,1,0:T(8,128)S(1)} %get-tuple-element.32), channel_id=1, source_target_pairs={{0,2},{1,3},{8,10},{9,11},{16,18},{17,19},{24,26},{25,27},{2,4},{3... | collective-permute-start | bytes 393224 | tf_op jit(solution)/shard_map/ppermute | solution.py:32

commit v3 on v0

v3 whole, which is shorter than its diff:
```python
import functools

import jax
import jax.numpy as jnp
from jax import lax
from jax.experimental import pallas as pl
from jax.experimental.pallas import tpu as pltpu
from jax.sharding import Mesh, PartitionSpec as P

AXES = ("y", "zh", "x", "zp", "zn", "c")
SIZES = (4, 2, 4, 2, 2, 2)
VMEM = pl.BlockSpec(memory_space=pltpu.VMEM)
f32 = functools.partial(jax.ShapeDtypeStruct, dtype=jnp.float32)
dot = functools.partial(jnp.dot, preferred_element_type=jnp.float32)
params = functools.partial(pltpu.CompilerParams, vmem_limit_bytes=24 << 20)


def split(value):
    high = value.astype(jnp.bfloat16)
    return high, (value - high.astype(jnp.float32)).astype(jnp.bfloat16)


def pack_kernel(at_ref, field_ref, packed_ref, sems):
    del at_ref
    copies = [
        pltpu.make_async_copy(field_ref.at[:, zh, :, q], packed_ref.at[:, :, q, zh], sems.at[4 * zh + q])
        for zh in range(2)
        for q in range(4)
    ]
    for copy in copies:
        copy.start()
    for copy in copies:
        copy.wait()


def pack(at, field):
    return pl.pallas_call(
        pack_kernel,
        in_specs=[pl.BlockSpec(memory_space=pltpu.SMEM), pl.BlockSpec(memory_space=pl.ANY)],
        out_specs=VMEM,
        out_shape=f32((4, 4, 4, 2, 2, 32, 128)),
        scratch_shapes=[pltpu.SemaphoreType.DMA((8,))],
        compiler_params=params(),
    )(at, field)


def contract_kernel(at_ref, x_ref, one_ref, two_ref, out_ref, reduced_ref):
    z = at_ref[0]
    high, low = split(one_ref[:, z // 4].reshape(512, 256).T)
    one = jnp.concatenate([high, high, low], axis=1)
    for t in range(4):
        block = jnp.concatenate([x_ref[:, q, t // 2, t % 2].reshape(512, 128) for q in range(4)], axis=1)
        high, low = split(block)
        high, low = split(dot(one, jnp.concatenate([high, low, high], axis=0)))
        reduced_ref[t] = jnp.concatenate([high, low, high], axis=1)
    high, low = split(two_ref[pl.ds(pl.multiple_of(z // 2 % 2 * 512, 512), 512)])
    partial = dot(reduced_ref[...].reshape(1024, 1536), jnp.concatenate([high, high, low], axis=0)).reshape(4, 256, 256)
    for t in range(4):
        for b in range(8):
            out_ref[t // 2 * 8 + b, t % 2] = partial[t, 32 * b:32 * b + 32]


def contract(at, received, basis_one, basis_two):
    return pl.pallas_call(
        contract_kernel,
        in_specs=[pl.BlockSpec(memory_space=pltpu.SMEM)] + [VMEM] * 3,
        out_specs=VMEM,
        out_shape=f32((16, 2, 32, 256)),
        scratch_shapes=[pltpu.VMEM((4, 256, 1536), jnp.bfloat16)],
        compiler_params=params(),
        cost_estimate=pl.CostEstimate(flops=4 * 3 * 2 * 256 * 256 * 1536, bytes_accessed=6 << 20, transcendentals=0),
    )(at, received, basis_one.reshape(4, 2, 4, 32, 256), basis_two)


def finish_kernel(part_ref, out_ref):
    for q in range(4):
        terms = [part_ref[zh, zp, q] for zh in range(2) for zp in range(2)]
        out_ref[2 * q:2 * q + 2] = (terms[0] + terms[1]) + (terms[2] + terms[3])


def finish(parts):
    return pl.pallas_call(
        finish_kernel, in_specs=[VMEM], out_specs=VMEM, out_shape=f32((8, 32, 256)), compiler_params=params()
    )(parts)


def on_device(species_field, basis_one, basis_two):
    z = lax.axis_index("zh") * 4 + lax.axis_index("zp") * 2
    at = z.astype(jnp.int32).reshape(1)
    packed = pack(at, species_field.reshape(4, 2, 4, 4, 2, 32, 128))
    moved = lax.all_to_all(packed.reshape(256, 32, 128), ("y", "x", "zn", "c"), split_axis=0, concat_axis=0, tiled=True)
    parts = contract(at, moved.reshape(16, 4, 2, 2, 32, 128), basis_one, basis_two)
    parts = lax.all_to_all(parts, ("zh", "zp", "zn", "c"), split_axis=0, concat_axis=0, tiled=True)
    return finish(parts.reshape(2, 2, 4, 2, 32, 256))


def solution(mesh):
    fine = Mesh(mesh.devices.reshape(SIZES), AXES)
    placed = (P(None, ("y", "zh", "x"), ("zp", "zn", "c")), P(), P())
    return jax.shard_map(
        on_device, mesh=fine, in_specs=placed, out_specs=P(("y", "zh", "x"), ("zp", "zn", "c"), None), check_vma=False
    )
```

time: 175 us -> 105 us (0.60)
  waiting for transfers between devices: 135 us -> 0 us
  blocking collectives: 0 us -> 98.6 us
  starting transfers between devices: 14.8 us -> 0 us
  between operations: 13.4 us -> 0.03 us
  matrix products: 6.77 us -> 0 us
  Pallas kernels: 0 us -> 3.97 us
    all_to_all x0 -> x2, blocking collectives: none -> 98.6 us  [the longest x1 62.3 us: on_device(): lax.all_to_all(packed.reshape(256, 32, 128), ('y', 'x', 'zn', 'c'), split...]
    all_to_all x1 -> x0, waiting for transfers between devices: 69.8 us -> none  [on_device(): lax.all_to_all(species_field, 'gx', split_axis=0, concat_axis=1, tiled=True)]
    reduce_scatter x1 -> x0, waiting for transfers between devices: 65.5 us -> none  [on_device(): lax.psum_scatter(partial_core, 'gy', scatter_dimension=1, tiled=True)]
    all_to_all x1 -> x0, starting transfers between devices: 14.8 us -> none  [on_device(): lax.all_to_all(species_field, 'gx', split_axis=0, concat_axis=1, tiled=True)]
    dot_general x2 -> x0, matrix products: 6.77 us -> none  [the longest x1 3.64 us: on_device(): jnp.einsum('kij,ir->krj', regrouped, basis_one, precision=lax.Precision.H...]
    pallas_call x0 -> x3, Pallas kernels: none -> 3.97 us  [the longest x1 2.85 us: contract(): pl.pallas_call(contract_kernel, in_specs=[pl.BlockSpec(memory_space=pltpu...]
    all_to_all x1 -> x0, local copies, waits for them, and re-layouts: 2.9 us -> none  [on_device(): lax.all_to_all(species_field, 'gx', split_axis=0, concat_axis=1, tiled=True)]
    unnamed x4 -> x6, local copies, waits for them, and re-layouts: 0.01 us -> 2.2 us
  transfers between devices with their start and end apart: 2 -> 0, of which waited for: 2 -> 0; matrix products, arithmetic and copies ran while one was open for 0% -> 0% of each run, Pallas kernels for 0% -> 0%
where the time goes in v3:
time: 105 us
  blocking collectives  98.6 us (94%)
  Pallas kernels  3.97 us (4%)
  local copies, waits for them, and re-layouts  2.2 us (2%)
    all_to_all x1, blocking collectives, on_device(): lax.all_to_all(packed.reshape(256, 32, 128), ('y', 'x', 'zn', 'c'), split...  62.3 us
    all_to_all x1, blocking collectives, on_device(): lax.all_to_all(parts, ('zh', 'zp', 'zn', 'c'), split_axis=0, concat_axis=...  36.3 us
    pallas_call x1, Pallas kernels, contract(): pl.pallas_call(contract_kernel, in_specs=[pl.BlockSpec(memory_space=pltpu...  2.85 us
    unnamed x6, local copies, waits for them, and re-layouts  2.2 us

profile of v3, /device:TPU:1, one launch (start us, length us, event | category | flops | bytes accessed | tf_op | source)
XLA Modules:
  0.0 104.9 jit_solution(6897515026432745185)
XLA Ops:
  0.0 0.0 copy-start
  0.0 2.2 %copy-done = f32[256,32,128]{2,1,0:T(8,128)S(1)} copy-done((f32[256,32,128]{2,1,0:T(8,128)S(1)}, f32[256,32,128]{2,1,0:T(8,128)}, u32[]{:S(2)}) %copy-start) | copy-done | bytes 4194328
  2.2 0.4 shard_map.37
  2.6 0.0 copy-start.1
  2.6 0.0 copy-start.2
  2.6 62.3 %all_to_all.10 = f32[256,32,128]{2,1,0:T(8,128)S(1)} all-to-all(f32[256,32,128]{2,1,0:T(8,128)S(1)} %bitcast.6), channel_id=1, replica_groups=mesh['y'=4,'zh'=2,'x'=4,'zp'=2,'zn'=2,'c'=2] {'y','x','zn','c'}, dimensions={0} | all-to-all | bytes 8388608 | tf_op jit(solution)/shard_map/all_to_all | solution.py:91
  64.9 0.0 copy-done.1
  64.9 0.0 copy-done.2
  64.9 2.9 %shard_map.38 = f32[16,2,32,256]{3,2,1,0:T(8,128)S(1)} custom-call(s32[1]{0:T(128)} %bitcast.at_ref, f32[16,4,2,2,32,128]{5,4,3,2,1,0:T(8,128)S(1)} %bitcast.9, f32[4,2,4,32,256]{4,3,2,1,0:T(8,128)S(1)} %bitcast.10, f32[1024,256]{1,0:T(8,128)S(1)} %copy-done.2), custom_call_target="tpu_custom_call" | custom-call | flops 2415919104 | bytes 6291456 | tf_op jit(solution)/shard_map/pallas_call | solution.py:64
  67.7 36.3 %all_to_all.11 = f32[16,2,32,256]{3,2,1,0:T(8,128)S(1)} all-to-all(f32[16,2,32,256]{3,2,1,0:T(8,128)S(1)} %shard_map.38), channel_id=1, replica_groups=mesh['y'=4,'zh'=2,'x'=4,'zp'=2,'zn'=2,'c'=2] {'zh','zp','zn','c'}, dimensions={0} | all-to-all | bytes 2097152 | tf_op jit(solution)/shard_map/all_to_all | solution.py:93
  104.1 0.8 shard_map.39
Async XLA Ops:
  0.0 2.2 %copy-start = (f32[256,32,128]{2,1,0:T(8,128)S(1)}, f32[256,32,128]{2,1,0:T(8,128)}, u32[]{:S(2)}) copy-start(f32[256,32,128]{2,1,0:T(8,128)} %param.3) | copy-start | bytes 12582916
  2.6 62.3 %copy-start.1 = (f32[1024,256]{1,0:T(8,128)S(1)}, f32[1024,256]{1,0:T(8,128)}, u32[]{:S(2)}) copy-start(f32[1024,256]{1,0:T(8,128)} %param.4) | copy-start | bytes 3145732
  2.6 62.3 %copy-start.2 = (f32[1024,256]{1,0:T(8,128)S(1)}, f32[1024,256]{1,0:T(8,128)}, u32[]{:S(2)}) copy-start(f32[1024,256]{1,0:T(8,128)} %two_ref.1) | copy-start | bytes 3145732

commit v4 on v3

v4 whole, which is shorter than its diff:
```python
import functools

import jax
import jax.numpy as jnp
from jax import lax
from jax.experimental import pallas as pl
from jax.experimental.pallas import tpu as pltpu
from jax.sharding import Mesh, PartitionSpec as P

AXES = ("y", "zh", "x", "zp", "zn", "c")
SIZES = (4, 2, 4, 2, 2, 2)
DISTANCES = (-2, 2, -3, 3, 4, -1, 1)
VMEM = pl.BlockSpec(memory_space=pltpu.VMEM)
SMEM = pl.BlockSpec(memory_space=pltpu.SMEM)
f32 = functools.partial(jax.ShapeDtypeStruct, dtype=jnp.float32)
dot = functools.partial(jnp.dot, preferred_element_type=jnp.float32)
params = functools.partial(pltpu.CompilerParams, vmem_limit_bytes=24 << 20)


def along(value, distance):
    pairs = []
    for y in range(4):
        for z in range(8):
            for x in range(4):
                for c in range(2):

                    def at(z):
                        return (((y * 2 + z // 4) * 4 + x) * 4 + z % 4) * 2 + c

                    pairs.append((at(z), at((z + distance) % 8)))
    return lax.ppermute(value, AXES, pairs)


def split(value):
    high = value.astype(jnp.bfloat16)
    return high, (value - high.astype(jnp.float32)).astype(jnp.bfloat16)


def pack_kernel(z_ref, core_ref, field_ref, packed_ref, sems):
    del z_ref, core_ref
    copies = [
        pltpu.make_async_copy(field_ref.at[:, zh, :, q], packed_ref.at[:, :, q, zh], sems.at[4 * zh + q])
        for zh in range(2)
        for q in range(4)
    ]
    for copy in copies:
        copy.start()
    for copy in copies:
        copy.wait()


def pack(z, core, field):
    return pl.pallas_call(
        pack_kernel,
        in_specs=[SMEM, SMEM, pl.BlockSpec(memory_space=pl.ANY)],
        out_specs=VMEM,
        out_shape=f32((4, 4, 4, 2, 2, 32, 128)),
        scratch_shapes=[pltpu.SemaphoreType.DMA((8,))],
        compiler_params=params(),
    )(z, core, field)


def contract_kernel(z_ref, core_ref, x_ref, one_ref, two_ref, out_ref, reduced_ref):
    z, core = z_ref[0], core_ref[0]
    high, low = split(one_ref[:, z // 4].reshape(512, 256).T)
    one = jnp.concatenate([high, high, low], axis=1)
    for t in range(4):
        block = jnp.concatenate([x_ref[:, q, t // 2, t % 2].reshape(512, 128) for q in range(4)], axis=1)
        high, low = split(block)
        high, low = split(dot(one, jnp.concatenate([high, low, high], axis=0)))
        reduced_ref[t] = jnp.concatenate([high, low, high], axis=1)
    high, low = split(two_ref[pl.ds(pl.multiple_of(z // 2 % 2 * 512, 512), 512)])
    partial = dot(reduced_ref[...].reshape(1024, 1536), jnp.concatenate([high, high, low], axis=0)).reshape(4, 256, 256)
    for t in range(4):
        for b in range(8):
            away = (4 * (t // 2) + b // 2 + 8 - z) % 8
            out_ref[away, (b % 2) ^ core, t % 2] = partial[t, 32 * b:32 * b + 32]


def contract(z, core, received, basis_one, basis_two):
    return pl.pallas_call(
        contract_kernel,
        in_specs=[SMEM] * 2 + [VMEM] * 3,
        out_specs=VMEM,
        out_shape=f32((8, 2, 2, 32, 256)),
        scratch_shapes=[pltpu.VMEM((4, 256, 1536), jnp.bfloat16)],
        compiler_params=params(),
        cost_estimate=pl.CostEstimate(flops=4 * 3 * 2 * 256 * 256 * 1536, bytes_accessed=6 << 20, transcendentals=0),
    )(z, core, received, basis_one.reshape(4, 2, 4, 32, 256), basis_two)


def add_kernel(first_ref, *refs):
    parts, (own_ref, other_ref) = dict(zip(DISTANCES, refs)), refs[7:]
    for core, out_ref in enumerate((own_ref, other_ref)):
        for odd in range(2):
            terms = [parts[d][core] for d in DISTANCES if d % 2 == odd]
            if not odd:
                terms.append(first_ref[0, core])
            out_ref[odd] = (terms[0] + terms[1]) + (terms[2] + terms[3])


def add(parts, received):
    return pl.pallas_call(
        add_kernel, in_specs=[VMEM] * 8, out_specs=[VMEM] * 2, out_shape=[f32((2, 2, 32, 256))] * 2, compiler_params=params()
    )(parts, *received)


def finish_kernel(z_ref, core_ref, own_ref, swapped_ref, out_ref):
    zn, core = z_ref[0] % 2, core_ref[0]
    for odd in range(2):
        out_ref[pl.ds(4 * (zn ^ odd) + 2 * core, 2)] = own_ref[odd]
        out_ref[pl.ds(4 * (zn ^ odd) + 2 - 2 * core, 2)] = swapped_ref[odd]


def finish(z, core, own, swapped):
    return pl.pallas_call(
        finish_kernel, in_specs=[SMEM] * 2 + [VMEM] * 2, out_specs=VMEM, out_shape=f32((8, 32, 256)), compiler_params=params()
    )(z, core, own, swapped)


def on_device(species_field, basis_one, basis_two):
    z = sum(lax.axis_index(axis) * size for axis, size in (("zh", 4), ("zp", 2), ("zn", 1))).astype(jnp.int32).reshape(1)
    core = lax.axis_index("c").astype(jnp.int32).reshape(1)
    packed = pack(z, core, species_field.reshape(4, 2, 4, 4, 2, 32, 128))
    moved = lax.all_to_all(packed.reshape(256, 32, 128), ("y", "x", "zn", "c"), split_axis=0, concat_axis=0, tiled=True)
    parts = contract(z, core, moved.reshape(16, 4, 2, 2, 32, 128), basis_one, basis_two)
    own, other = add(parts[:1], [along(parts[distance % 8], distance) for distance in DISTANCES])
    return finish(z, core, own, lax.ppermute(other, "c", [(0, 1), (1, 0)]))


def solution(mesh):
    fine = Mesh(mesh.devices.reshape(SIZES), AXES)
    placed = (P(None, ("y", "zh", "x"), ("zp", "zn", "c")), P(), P())
    return jax.shard_map(
        on_device, mesh=fine, in_specs=placed, out_specs=P(("y", "zh", "x"), ("zp", "zn", "c"), None), check_vma=False
    )
```

time: 105 us -> 100 us (0.952)
  blocking collectives: 98.6 us -> 62.3 us
  starting transfers between devices: 0 us -> 18.7 us
  waiting for transfers between devices: 0 us -> 11.8 us
    all_to_all x1 -> x0, blocking collectives: 36.3 us -> none  [on_device(): lax.all_to_all(parts, ('zh', 'zp', 'zn', 'c'), split_axis=0, concat_axis=...]
    ppermute x0 -> x8, starting transfers between devices: none -> 18.7 us  [the longest x7 16.8 us: along(): return lax.ppermute(value, AXES, pairs)]
    ppermute x0 -> x8, waiting for transfers between devices: none -> 11.8 us  [the longest x7 10.8 us: along(): return lax.ppermute(value, AXES, pairs)]
    pallas_call x3 -> x4, Pallas kernels: 3.97 us -> 4.02 us  [the longest x1 2.87 us: contract(): pl.pallas_call(contract_kernel, in_specs=[SMEM] * 2 + [VMEM] * 3, out_spe...]
  transfers between devices with their start and end apart: 0 -> 8, of which waited for: 0 -> 3; matrix products, arithmetic and copies ran while one was open for 0% -> 0% of each run, Pallas kernels for 0% -> 0%
where the time goes in v4:
time: 100 us; the launch traced here: 99.2 us
  blocking collectives  62.3 us (62%)
  starting transfers between devices  18.7 us (19%)
  waiting for transfers between devices  11.8 us (12%)
  Pallas kernels  4.02 us (4%)
  local copies, waits for them, and re-layouts  2.3 us (2%)
    all_to_all x1, blocking collectives, on_device(): lax.all_to_all(packed.reshape(256, 32, 128), ('y', 'x', 'zn', 'c'), split...  62.3 us
    ppermute x7, starting transfers between devices, along(): return lax.ppermute(value, AXES, pairs)  16.8 us
    ppermute x7, waiting for transfers between devices, along(): return lax.ppermute(value, AXES, pairs)  10.8 us
    pallas_call x1, Pallas kernels, contract(): pl.pallas_call(contract_kernel, in_specs=[SMEM] * 2 + [VMEM] * 3, out_spe...  2.87 us
    unnamed x6, local copies, waits for them, and re-layouts  2.2 us
  transfers between devices with their start and end apart: 8, of which 3 were waited for; matrix products, arithmetic and copies ran while one was open for 0% of the time, Pallas kernels for 0%

profile of v4, /device:TPU:1, one launch (start us, length us, event | category | flops | bytes accessed | tf_op | source)
XLA Modules:
  0.0 99.2 jit_solution(15218214134067624514)
XLA Ops:
  0.0 0.0 copy-start
  0.0 2.2 %copy-done = f32[256,32,128]{2,1,0:T(8,128)S(1)} copy-done((f32[256,32,128]{2,1,0:T(8,128)S(1)}, f32[256,32,128]{2,1,0:T(8,128)}, u32[]{:S(2)}) %copy-start) | copy-done | bytes 4194328
  2.2 0.4 shard_map.37
  2.6 0.0 copy-start.1
  2.6 0.0 copy-start.2
  2.6 62.3 %all_to_all.5 = f32[256,32,128]{2,1,0:T(8,128)S(1)} all-to-all(f32[256,32,128]{2,1,0:T(8,128)S(1)} %bitcast.20), channel_id=1, replica_groups=mesh['y'=4,'zh'=2,'x'=4,'zp'=2,'zn'=2,'c'=2] {'y','x','zn','c'}, dimensions={0} | all-to-all | bytes 8388608 | tf_op jit(solution)/shard_map/all_to_all | solution.py:125
  64.9 0.0 copy-done.1
  64.9 0.0 copy-done.2
  64.9 2.9 %shard_map.38 = f32[8,2,2,32,256]{4,3,2,1,0:T(8,128)S(1)} custom-call(s32[1]{0:T(128)} %bitcast.z_ref, s32[1]{0:T(128)} %bitcast.1.core_ref, f32[16,4,2,2,32,128]{5,4,3,2,1,0:T(8,128)S(1)} %bitcast.22, f32[4,2,4,32,256]{4,3,2,1,0:T(8,128)S(1)} %bitcast.23, f32[1024,256]{1,0:T(8,128)S(1)} %copy-done.2), custom_call_target="tpu_custom_call" | custom-call | flops 2415919104 | bytes 6291456 | tf_op jit(solution)/shard_map/pallas_call | solution.py:81
  67.8 0.1 slice_bitcast_fusion
  67.9 0.1 collective-permute-start.6
  68.0 2.8 %collective-permute-start.5 = (f32[2,2,32,256]{3,2,1,0:T(8,128)S(1)}, f32[2,2,32,256]{3,2,1,0:T(8,128)S(1)}, u32[]{:S(2)}, u32[]{:S(2)}) collective-permute-start(f32[2,2,32,256]{3,2,1,0:T(8,128)S(1)} %get-tuple-element.10), channel_id=1, source_target_pairs={{0,38},{1,39},{8,46},{9,47},{16,54},{17,55},{24,62},{25,63},{2,0},... | collective-permute-start | bytes 393224 | tf_op jit(solution)/shard_map/ppermute | solution.py:31
  70.7 5.9 %collective-permute-start.4 = (f32[2,2,32,256]{3,2,1,0:T(8,128)S(1)}, f32[2,2,32,256]{3,2,1,0:T(8,128)S(1)}, u32[]{:S(2)}, u32[]{:S(2)}) collective-permute-start(f32[2,2,32,256]{3,2,1,0:T(8,128)S(1)} %get-tuple-element.11), channel_id=1, source_target_pairs={{0,32},{1,33},{8,40},{9,41},{16,48},{17,49},{24,56},{25,57},{2,34}... | collective-permute-start | bytes 393224 | tf_op jit(solution)/shard_map/ppermute | solution.py:31
  76.7 0.0 collective-permute-start.3
  76.7 4.5 %collective-permute-start.2 = (f32[2,2,32,256]{3,2,1,0:T(8,128)S(1)}, f32[2,2,32,256]{3,2,1,0:T(8,128)S(1)}, u32[]{:S(2)}, u32[]{:S(2)}) collective-permute-start(f32[2,2,32,256]{3,2,1,0:T(8,128)S(1)} %get-tuple-element.13), channel_id=1, source_target_pairs={{0,34},{1,35},{8,42},{9,43},{16,50},{17,51},{24,58},{25,59},{2,36}... | collective-permute-start | bytes 393224 | tf_op jit(solution)/shard_map/ppermute | solution.py:31
  81.1 0.0 collective-permute-done.6.refs_6_
  81.1 0.0 collective-permute-start.1
  81.1 0.0 collective-permute-done.5.refs_5_
  81.1 3.6 %collective-permute-start = (f32[2,2,32,256]{3,2,1,0:T(8,128)S(1)}, f32[2,2,32,256]{3,2,1,0:T(8,128)S(1)}, u32[]{:S(2)}, u32[]{:S(2)}) collective-permute-start(f32[2,2,32,256]{3,2,1,0:T(8,128)S(1)} %get-tuple-element.15), channel_id=1, source_target_pairs={{0,36},{1,37},{8,44},{9,45},{16,52},{17,53},{24,60},{25,61},{2,38}... | collective-permute-start | bytes 393224 | tf_op jit(solution)/shard_map/ppermute | solution.py:31
  84.7 0.0 collective-permute-done.4.refs_4_
  84.7 8.5 %collective-permute-done.3.refs_3_ = f32[2,2,32,256]{3,2,1,0:T(8,128)S(1)} collective-permute-done((f32[2,2,32,256]{3,2,1,0:T(8,128)S(1)}, f32[2,2,32,256]{3,2,1,0:T(8,128)S(1)}, u32[]{:S(2)}, u32[]{:S(2)}) %collective-permute-start.3) | collective-permute-done | bytes 131104 | tf_op jit(solution)/shard_map/ppermute | solution.py:31
  93.2 0.0 collective-permute-done.2.refs_2_
  93.2 0.0 collective-permute-done.1.refs_1_
  93.2 2.3 %collective-permute-done.refs_0_ = f32[2,2,32,256]{3,2,1,0:T(8,128)S(1)} collective-permute-done((f32[2,2,32,256]{3,2,1,0:T(8,128)S(1)}, f32[2,2,32,256]{3,2,1,0:T(8,128)S(1)}, u32[]{:S(2)}, u32[]{:S(2)}) %collective-permute-start) | collective-permute-done | bytes 131104 | tf_op jit(solution)/shard_map/ppermute | solution.py:31
  95.5 0.1 shard_map.39
  95.5 1.9 %collective-permute-start.7 = (f32[2,2,32,256]{3,2,1,0:T(8,128)S(1)}, f32[2,2,32,256]{3,2,1,0:T(8,128)S(1)}, u32[]{:S(2)}, u32[]{:S(2)}) collective-permute-start(f32[2,2,32,256]{3,2,1,0:T(8,128)S(1)} %get-tuple-element.8), channel_id=1, source_target_pairs={{0,1},{1,0},{2,3},{3,2},{4,5},{5,4},{6,7},{7,6},{8,9},{9,8},{10,11... | collective-permute-start | bytes 393224 | tf_op jit(solution)/shard_map/ppermute | solution.py:128
  97.5 1.0 collective-permute-done.7.swapped_ref
  98.4 0.7 shard_map.40
Async XLA Ops:
  0.0 2.2 %copy-start = (f32[256,32,128]{2,1,0:T(8,128)S(1)}, f32[256,32,128]{2,1,0:T(8,128)}, u32[]{:S(2)}) copy-start(f32[256,32,128]{2,1,0:T(8,128)} %param.3) | copy-start | bytes 12582916
  2.6 62.3 %copy-start.1 = (f32[1024,256]{1,0:T(8,128)S(1)}, f32[1024,256]{1,0:T(8,128)}, u32[]{:S(2)}) copy-start(f32[1024,256]{1,0:T(8,128)} %param.4) | copy-start | bytes 3145732
  2.6 62.3 %copy-start.2 = (f32[1024,256]{1,0:T(8,128)S(1)}, f32[1024,256]{1,0:T(8,128)}, u32[]{:S(2)}) copy-start(f32[1024,256]{1,0:T(8,128)} %two_ref.1) | copy-start | bytes 3145732
  67.9 13.2 %collective-permute-start.6 = (f32[2,2,32,256]{3,2,1,0:T(8,128)S(1)}, f32[2,2,32,256]{3,2,1,0:T(8,128)S(1)}, u32[]{:S(2)}, u32[]{:S(2)}) collective-permute-start(f32[2,2,32,256]{3,2,1,0:T(8,128)S(1)} %get-tuple-element.9), channel_id=1, source_target_pairs={{0,2},{1,3},{8,10},{9,11},{16,18},{17,19},{24,26},{25,27},{2,4},{3... | collective-permute-start | bytes 393224 | tf_op jit(solution)/shard_map/ppermute | solution.py:31
  68.0 13.2 %collective-permute-start.5 = (f32[2,2,32,256]{3,2,1,0:T(8,128)S(1)}, f32[2,2,32,256]{3,2,1,0:T(8,128)S(1)}, u32[]{:S(2)}, u32[]{:S(2)}) collective-permute-start(f32[2,2,32,256]{3,2,1,0:T(8,128)S(1)} %get-tuple-element.10), channel_id=1, source_target_pairs={{0,38},{1,39},{8,46},{9,47},{16,54},{17,55},{24,62},{25,63},{2,0},... | collective-permute-start | bytes 393224 | tf_op jit(solution)/shard_map/ppermute | solution.py:31
  70.7 14.0 %collective-permute-start.4 = (f32[2,2,32,256]{3,2,1,0:T(8,128)S(1)}, f32[2,2,32,256]{3,2,1,0:T(8,128)S(1)}, u32[]{:S(2)}, u32[]{:S(2)}) collective-permute-start(f32[2,2,32,256]{3,2,1,0:T(8,128)S(1)} %get-tuple-element.11), channel_id=1, source_target_pairs={{0,32},{1,33},{8,40},{9,41},{16,48},{17,49},{24,56},{25,57},{2,34}... | collective-permute-start | bytes 393224 | tf_op jit(solution)/shard_map/ppermute | solution.py:31
  76.7 16.5 %collective-permute-start.3 = (f32[2,2,32,256]{3,2,1,0:T(8,128)S(1)}, f32[2,2,32,256]{3,2,1,0:T(8,128)S(1)}, u32[]{:S(2)}, u32[]{:S(2)}) collective-permute-start(f32[2,2,32,256]{3,2,1,0:T(8,128)S(1)} %get-tuple-element.12), channel_id=1, source_target_pairs={{0,6},{1,7},{8,14},{9,15},{16,22},{17,23},{24,30},{25,31},{2,32},{... | collective-permute-start | bytes 393224 | tf_op jit(solution)/shard_map/ppermute | solution.py:31
  76.7 16.5 %collective-permute-start.2 = (f32[2,2,32,256]{3,2,1,0:T(8,128)S(1)}, f32[2,2,32,256]{3,2,1,0:T(8,128)S(1)}, u32[]{:S(2)}, u32[]{:S(2)}) collective-permute-start(f32[2,2,32,256]{3,2,1,0:T(8,128)S(1)} %get-tuple-element.13), channel_id=1, source_target_pairs={{0,34},{1,35},{8,42},{9,43},{16,50},{17,51},{24,58},{25,59},{2,36}... | collective-permute-start | bytes 393224 | tf_op jit(solution)/shard_map/ppermute | solution.py:31
  81.1 12.0 %collective-permute-start.1 = (f32[2,2,32,256]{3,2,1,0:T(8,128)S(1)}, f32[2,2,32,256]{3,2,1,0:T(8,128)S(1)}, u32[]{:S(2)}, u32[]{:S(2)}) collective-permute-start(f32[2,2,32,256]{3,2,1,0:T(8,128)S(1)} %get-tuple-element.14), channel_id=1, source_target_pairs={{0,4},{1,5},{8,12},{9,13},{16,20},{17,21},{24,28},{25,29},{2,6},{3... | collective-permute-start | bytes 393224 | tf_op jit(solution)/shard_map/ppermute | solution.py:31
  81.1 14.3 %collective-permute-start = (f32[2,2,32,256]{3,2,1,0:T(8,128)S(1)}, f32[2,2,32,256]{3,2,1,0:T(8,128)S(1)}, u32[]{:S(2)}, u32[]{:S(2)}) collective-permute-start(f32[2,2,32,256]{3,2,1,0:T(8,128)S(1)} %get-tuple-element.15), channel_id=1, source_target_pairs={{0,36},{1,37},{8,44},{9,45},{16,52},{17,53},{24,60},{25,61},{2,38}... | collective-permute-start | bytes 393224 | tf_op jit(solution)/shard_map/ppermute | solution.py:31
  95.5 2.9 %collective-permute-start.7 = (f32[2,2,32,256]{3,2,1,0:T(8,128)S(1)}, f32[2,2,32,256]{3,2,1,0:T(8,128)S(1)}, u32[]{:S(2)}, u32[]{:S(2)}) collective-permute-start(f32[2,2,32,256]{3,2,1,0:T(8,128)S(1)} %get-tuple-element.8), channel_id=1, source_target_pairs={{0,1},{1,0},{2,3},{3,2},{4,5},{5,4},{6,7},{7,6},{8,9},{9,8},{10,11... | collective-permute-start | bytes 393224 | tf_op jit(solution)/shard_map/ppermute | solution.py:128

commit v5 on v4

v5 whole, which is shorter than its diff:
```python
import functools

import jax
import jax.numpy as jnp
from jax import lax
from jax.experimental import pallas as pl
from jax.experimental.pallas import tpu as pltpu
from jax.sharding import Mesh, PartitionSpec as P

AXES = ("y", "zh", "x", "zp", "zn", "c")
SIZES = (4, 2, 4, 2, 2, 2)
FIRST = (1, 2, 4, 7)
SENDS = ((1, 2, 3, 0), (0, 3, 2, 1), (2, 1, 0, 3), (3, 0, 1, 2))
TARGETS = [dict(zip(FIRST, to)) | {7 - z: 7 - t for z, t in zip(FIRST, to)} for to in SENDS]
ORDER = (1, 3, 2, 0)
VMEM = pl.BlockSpec(memory_space=pltpu.VMEM)
SMEM = pl.BlockSpec(memory_space=pltpu.SMEM)
f32 = functools.partial(jax.ShapeDtypeStruct, dtype=jnp.float32)
dot = functools.partial(jnp.dot, preferred_element_type=jnp.float32)
params = functools.partial(pltpu.CompilerParams, vmem_limit_bytes=24 << 20)


def send(value, number):
    pairs = []
    for y in range(4):
        for z in range(8):
            for x in range(4):
                for c in range(2):

                    def at(z):
                        return (((y * 2 + z // 4) * 4 + x) * 4 + z % 4) * 2 + c

                    pairs.append((at(z), at(TARGETS[number][z])))
    return lax.ppermute(value, AXES, pairs)


def split(value):
    high = value.astype(jnp.bfloat16)
    return high, (value - high.astype(jnp.float32)).astype(jnp.bfloat16)


def pack_kernel(z_ref, core_ref, field_ref, packed_ref, sems):
    del core_ref
    first = 1 - (z_ref[0] // 4 ^ z_ref[0] // 2 % 2)
    copies = [
        pltpu.make_async_copy(field_ref.at[:, first ^ zn, :, c], packed_ref.at[:, :, zn, c], sems.at[2 * zn + c])
        for zn in range(2)
        for c in range(2)
    ]
    for copy in copies:
        copy.start()
    for copy in copies:
        copy.wait()


def pack(z, core, field):
    return pl.pallas_call(
        pack_kernel,
        in_specs=[SMEM, SMEM, pl.BlockSpec(memory_space=pl.ANY)],
        out_specs=VMEM,
        out_shape=f32((4, 4, 2, 2, 4, 32, 128)),
        scratch_shapes=[pltpu.SemaphoreType.DMA((4,))],
        compiler_params=params(),
    )(z, core, field)


def contract_kernel(z_ref, core_ref, x_ref, one_ref, two_ref, out_ref, reduced_ref):
    z, core = z_ref[0], core_ref[0]
    high, low = split(one_ref[:, z // 4].reshape(512, 256).T)
    one = jnp.concatenate([high, high, low], axis=1)
    for t in range(4):
        block = jnp.concatenate([x_ref[:, q, t].reshape(512, 128) for q in range(4)], axis=1)
        high, low = split(block)
        high, low = split(dot(one, jnp.concatenate([high, low, high], axis=0)))
        reduced_ref[t] = jnp.concatenate([high, low, high], axis=1)
    high, low = split(two_ref[pl.ds(pl.multiple_of(z // 2 % 2 * 512, 512), 512)])
    partial = dot(reduced_ref[...].reshape(1024, 1536), jnp.concatenate([high, high, low], axis=0)).reshape(4, 256, 256)
    for b in range(8):
        table = sum(n << 2 * chip for n in range(4) for chip, to in TARGETS[n].items() if to % 4 == b // 2)
        number = (table >> 2 * z) & 3
        for t in range(4):
            out_ref[number, (b % 2) ^ core, t] = partial[t, 32 * b:32 * b + 32]


def contract(z, core, received, basis_one, basis_two):
    return pl.pallas_call(
        contract_kernel,
        in_specs=[SMEM] * 2 + [VMEM] * 3,
        out_specs=VMEM,
        out_shape=f32((4, 2, 4, 32, 256)),
        scratch_shapes=[pltpu.VMEM((4, 256, 1536), jnp.bfloat16)],
        compiler_params=params(),
        cost_estimate=pl.CostEstimate(flops=4 * 3 * 2 * 256 * 256 * 1536, bytes_accessed=6 << 20, transcendentals=0),
    )(z, core, received, basis_one.reshape(4, 2, 4, 32, 256), basis_two)


def add_kernel(a_ref, b_ref, c_ref, d_ref, own_ref, other_ref):
    for core, out_ref in enumerate((own_ref, other_ref)):
        out_ref[...] = (a_ref[core] + b_ref[core]) + (c_ref[core] + d_ref[core])


def add(received):
    return pl.pallas_call(
        add_kernel, in_specs=[VMEM] * 4, out_specs=[VMEM] * 2, out_shape=[f32((4, 32, 256))] * 2, compiler_params=params()
    )(*received)


def finish_kernel(core_ref, own_ref, swapped_ref, out_ref):
    core = core_ref[0]
    out_ref[pl.ds(4 * core, 4)] = own_ref[...]
    out_ref[pl.ds(4 - 4 * core, 4)] = swapped_ref[...]


def finish(core, own, swapped):
    return pl.pallas_call(
        finish_kernel, in_specs=[SMEM, VMEM, VMEM], out_specs=VMEM, out_shape=f32((8, 32, 256)), compiler_params=params()
    )(core, own, swapped)


def on_device(species_field, basis_one, basis_two):
    z = sum(lax.axis_index(axis) * size for axis, size in (("zh", 4), ("zp", 2), ("zn", 1))).astype(jnp.int32).reshape(1)
    core = lax.axis_index("c").astype(jnp.int32).reshape(1)
    packed = pack(z, core, species_field.reshape(4, 2, 4, 2, 4, 32, 128))
    moved = lax.all_to_all(packed.reshape(256, 32, 128), ("y", "x", "zn", "c"), split_axis=0, concat_axis=0, tiled=True)
    parts = contract(z, core, moved.reshape(16, 4, 4, 32, 128), basis_one, basis_two)
    own, other = add([send(parts[number], number) for number in ORDER])
    return finish(core, own, lax.ppermute(other, "c", [(0, 1), (1, 0)]))


def solution(mesh):
    fine = Mesh(mesh.devices.reshape(SIZES), AXES)
    placed = (P(None, ("y", "zh", "x"), ("zp", "zn", "c")), P(), P())
    return jax.shard_map(
        on_device, mesh=fine, in_specs=placed, out_specs=P(("y", "zh", "x"), ("zp", "zn", "c"), None), check_vma=False
    )
```

time: 100 us -> 98.4 us (0.984)
  starting transfers between devices: 18.7 us -> 11.4 us
  waiting for transfers between devices: 11.8 us -> 17.6 us
    ppermute x8 -> x5, starting transfers between devices: 18.7 us -> 11.4 us  [the longest x4 10.3 us: send(): return lax.ppermute(value, AXES, pairs)]
    ppermute x8 -> x5, waiting for transfers between devices: 11.8 us -> 17.6 us  [the longest x4 16.6 us: send(): return lax.ppermute(value, AXES, pairs)]
  transfers between devices with their start and end apart: 8 -> 5, of which waited for: 3 -> 3; matrix products, arithmetic and copies ran while one was open for 0% -> 0% of each run, Pallas kernels for 0% -> 0%
where the time goes in v5:
time: 98.4 us; the launch traced here: 97.6 us
  blocking collectives  62.3 us (63%)
  waiting for transfers between devices  17.6 us (18%)
  starting transfers between devices  11.4 us (12%)
  Pallas kernels  3.97 us (4%)
  local copies, waits for them, and re-layouts  2.3 us (2%)
    all_to_all x1, blocking collectives, on_device(): lax.all_to_all(packed.reshape(256, 32, 128), ('y', 'x', 'zn', 'c'), split...  62.3 us
    ppermute x4, waiting for transfers between devices, send(): return lax.ppermute(value, AXES, pairs)  16.6 us
    ppermute x4, starting transfers between devices, send(): return lax.ppermute(value, AXES, pairs)  10.3 us
    pallas_call x1, Pallas kernels, contract(): pl.pallas_call(contract_kernel, in_specs=[SMEM] * 2 + [VMEM] * 3, out_spe...  2.88 us
    unnamed x6, local copies, waits for them, and re-layouts  2.2 us
  transfers between devices with their start and end apart: 5, of which 3 were waited for; matrix products, arithmetic and copies ran while one was open for 0% of the time, Pallas kernels for 0%

profile of v5, /device:TPU:1, one launch (start us, length us, event | category | flops | bytes accessed | tf_op | source)
XLA Modules:
  0.0 97.6 jit_solution(4996438253688401197)
XLA Ops:
  0.0 0.0 copy-start
  0.0 2.2 %copy-done = f32[256,32,128]{2,1,0:T(8,128)S(1)} copy-done((f32[256,32,128]{2,1,0:T(8,128)S(1)}, f32[256,32,128]{2,1,0:T(8,128)}, u32[]{:S(2)}) %copy-start) | copy-done | bytes 4194328
  2.2 0.3 shard_map.37
  2.5 0.0 copy-start.1
  2.5 0.0 copy-start.2
  2.5 62.3 %all_to_all.5 = f32[256,32,128]{2,1,0:T(8,128)S(1)} all-to-all(f32[256,32,128]{2,1,0:T(8,128)S(1)} %bitcast.14), channel_id=1, replica_groups=mesh['y'=4,'zh'=2,'x'=4,'zp'=2,'zn'=2,'c'=2] {'y','x','zn','c'}, dimensions={0} | all-to-all | bytes 8388608 | tf_op jit(solution)/shard_map/all_to_all | solution.py:124
  64.8 0.0 copy-done.1
  64.8 0.0 copy-done.2
  64.8 2.9 %shard_map.38 = f32[4,2,4,32,256]{4,3,2,1,0:T(8,128)S(1)} custom-call(s32[1]{0:T(128)} %bitcast.1.z_ref, s32[1]{0:T(128)} %bitcast.core_ref, f32[16,4,4,32,128]{4,3,2,1,0:T(8,128)S(1)} %bitcast.16, f32[4,2,4,32,256]{4,3,2,1,0:T(8,128)S(1)} %bitcast.17, f32[1024,256]{1,0:T(8,128)S(1)} %copy-done.2), custom_call_target="tpu_custom_call" | custom-call | flops 2415919104 | bytes 6291456 | tf_op jit(solution)/shard_map/pallas_call | solution.py:86
  67.7 0.1 slice_bitcast_fusion
  67.8 4.6 %collective-permute-start.3 = (f32[2,4,32,256]{3,2,1,0:T(8,128)S(1)}, f32[2,4,32,256]{3,2,1,0:T(8,128)S(1)}, u32[]{:S(2)}, u32[]{:S(2)}) collective-permute-start(f32[2,4,32,256]{3,2,1,0:T(8,128)S(1)} %get-tuple-element.9), channel_id=1, source_target_pairs={{0,38},{1,39},{8,46},{9,47},{16,54},{17,55},{24,62},{25,63},{2,2},... | collective-permute-start | bytes 786440 | tf_op jit(solution)/shard_map/ppermute | solution.py:34
  72.4 3.4 %collective-permute-start.2 = (f32[2,4,32,256]{3,2,1,0:T(8,128)S(1)}, f32[2,4,32,256]{3,2,1,0:T(8,128)S(1)}, u32[]{:S(2)}, u32[]{:S(2)}) collective-permute-start(f32[2,4,32,256]{3,2,1,0:T(8,128)S(1)} %get-tuple-element.10), channel_id=1, source_target_pairs={{0,32},{1,33},{8,40},{9,41},{16,48},{17,49},{24,56},{25,57},{2,4},... | collective-permute-start | bytes 786440 | tf_op jit(solution)/shard_map/ppermute | solution.py:34
  75.9 0.0 collective-permute-start.1
  75.9 2.3 %collective-permute-start = (f32[2,4,32,256]{3,2,1,0:T(8,128)S(1)}, f32[2,4,32,256]{3,2,1,0:T(8,128)S(1)}, u32[]{:S(2)}, u32[]{:S(2)}) collective-permute-start(f32[2,4,32,256]{3,2,1,0:T(8,128)S(1)} %get-tuple-element.12), channel_id=1, source_target_pairs={{0,36},{1,37},{8,44},{9,45},{16,52},{17,53},{24,60},{25,61},{2,0},... | collective-permute-start | bytes 786440 | tf_op jit(solution)/shard_map/ppermute | solution.py:34
  78.2 0.0 collective-permute-done.3.d_ref
  78.2 4.2 %collective-permute-done.2.c_ref = f32[2,4,32,256]{3,2,1,0:T(8,128)S(1)} collective-permute-done((f32[2,4,32,256]{3,2,1,0:T(8,128)S(1)}, f32[2,4,32,256]{3,2,1,0:T(8,128)S(1)}, u32[]{:S(2)}, u32[]{:S(2)}) %collective-permute-start.2) | collective-permute-done | bytes 262176 | tf_op jit(solution)/shard_map/ppermute | solution.py:34
  82.4 12.4 %collective-permute-done.1.b_ref = f32[2,4,32,256]{3,2,1,0:T(8,128)S(1)} collective-permute-done((f32[2,4,32,256]{3,2,1,0:T(8,128)S(1)}, f32[2,4,32,256]{3,2,1,0:T(8,128)S(1)}, u32[]{:S(2)}, u32[]{:S(2)}) %collective-permute-start.1) | collective-permute-done | bytes 262176 | tf_op jit(solution)/shard_map/ppermute | solution.py:34
  94.8 0.0 collective-permute-done.a_ref
  94.8 0.1 shard_map.39
  94.8 1.1 %collective-permute-start.4 = (f32[4,32,256]{2,1,0:T(8,128)S(1)}, f32[4,32,256]{2,1,0:T(8,128)S(1)}, u32[]{:S(2)}, u32[]{:S(2)}) collective-permute-start(f32[4,32,256]{2,1,0:T(8,128)S(1)} %get-tuple-element.8), channel_id=1, source_target_pairs={{0,1},{1,0},{2,3},{3,2},{4,5},{5,4},{6,7},{7,6},{8,9},{9,8},{10,11... | collective-permute-start | bytes 393224 | tf_op jit(solution)/shard_map/ppermute | solution.py:127
  95.9 1.0 %collective-permute-done.4.swapped_ref = f32[4,32,256]{2,1,0:T(8,128)S(1)} collective-permute-done((f32[4,32,256]{2,1,0:T(8,128)S(1)}, f32[4,32,256]{2,1,0:T(8,128)S(1)}, u32[]{:S(2)}, u32[]{:S(2)}) %collective-permute-start.4) | collective-permute-done | bytes 131104 | tf_op jit(solution)/shard_map/ppermute | solution.py:127
  96.9 0.7 shard_map.40
Async XLA Ops:
  0.0 2.2 %copy-start = (f32[256,32,128]{2,1,0:T(8,128)S(1)}, f32[256,32,128]{2,1,0:T(8,128)}, u32[]{:S(2)}) copy-start(f32[256,32,128]{2,1,0:T(8,128)} %param.3) | copy-start | bytes 12582916
  2.5 62.3 %copy-start.1 = (f32[1024,256]{1,0:T(8,128)S(1)}, f32[1024,256]{1,0:T(8,128)}, u32[]{:S(2)}) copy-start(f32[1024,256]{1,0:T(8,128)} %param.4) | copy-start | bytes 3145732
  2.5 62.3 %copy-start.2 = (f32[1024,256]{1,0:T(8,128)S(1)}, f32[1024,256]{1,0:T(8,128)}, u32[]{:S(2)}) copy-start(f32[1024,256]{1,0:T(8,128)} %two_ref.1) | copy-start | bytes 3145732
  67.8 10.3 %collective-permute-start.3 = (f32[2,4,32,256]{3,2,1,0:T(8,128)S(1)}, f32[2,4,32,256]{3,2,1,0:T(8,128)S(1)}, u32[]{:S(2)}, u32[]{:S(2)}) collective-permute-start(f32[2,4,32,256]{3,2,1,0:T(8,128)S(1)} %get-tuple-element.9), channel_id=1, source_target_pairs={{0,38},{1,39},{8,46},{9,47},{16,54},{17,55},{24,62},{25,63},{2,2},... | collective-permute-start | bytes 786440 | tf_op jit(solution)/shard_map/ppermute | solution.py:34
  72.4 9.9 %collective-permute-start.2 = (f32[2,4,32,256]{3,2,1,0:T(8,128)S(1)}, f32[2,4,32,256]{3,2,1,0:T(8,128)S(1)}, u32[]{:S(2)}, u32[]{:S(2)}) collective-permute-start(f32[2,4,32,256]{3,2,1,0:T(8,128)S(1)} %get-tuple-element.10), channel_id=1, source_target_pairs={{0,32},{1,33},{8,40},{9,41},{16,48},{17,49},{24,56},{25,57},{2,4},... | collective-permute-start | bytes 786440 | tf_op jit(solution)/shard_map/ppermute | solution.py:34
  75.9 18.9 %collective-permute-start.1 = (f32[2,4,32,256]{3,2,1,0:T(8,128)S(1)}, f32[2,4,32,256]{3,2,1,0:T(8,128)S(1)}, u32[]{:S(2)}, u32[]{:S(2)}) collective-permute-start(f32[2,4,32,256]{3,2,1,0:T(8,128)S(1)} %get-tuple-element.11), channel_id=1, source_target_pairs={{0,34},{1,35},{8,42},{9,43},{16,50},{17,51},{24,58},{25,59},{2,6},... | collective-permute-start | bytes 786440 | tf_op jit(solution)/shard_map/ppermute | solution.py:34
  75.9 18.9 %collective-permute-start = (f32[2,4,32,256]{3,2,1,0:T(8,128)S(1)}, f32[2,4,32,256]{3,2,1,0:T(8,128)S(1)}, u32[]{:S(2)}, u32[]{:S(2)}) collective-permute-start(f32[2,4,32,256]{3,2,1,0:T(8,128)S(1)} %get-tuple-element.12), channel_id=1, source_target_pairs={{0,36},{1,37},{8,44},{9,45},{16,52},{17,53},{24,60},{25,61},{2,0},... | collective-permute-start | bytes 786440 | tf_op jit(solution)/shard_map/ppermute | solution.py:34
  94.8 2.1 %collective-permute-start.4 = (f32[4,32,256]{2,1,0:T(8,128)S(1)}, f32[4,32,256]{2,1,0:T(8,128)S(1)}, u32[]{:S(2)}, u32[]{:S(2)}) collective-permute-start(f32[4,32,256]{2,1,0:T(8,128)S(1)} %get-tuple-element.8), channel_id=1, source_target_pairs={{0,1},{1,0},{2,3},{3,2},{4,5},{5,4},{6,7},{7,6},{8,9},{9,8},{10,11... | collective-permute-start | bytes 393224 | tf_op jit(solution)/shard_map/ppermute | solution.py:127

commit v6 on v5

--- a/solution.py
+++ b/solution.py
@@ -20,17 +20,22 @@
 params = functools.partial(pltpu.CompilerParams, vmem_limit_bytes=24 << 20)
 
 
+def device(y, z, x, c):
+    return (((y * 2 + z // 4) * 4 + x) * 4 + z % 4) * 2 + c
+
+
+def groups():
+    halves = [sorted((z, z + 1), key=lambda chip: chip not in FIRST) for z in range(0, 8, 2)]
+    return [[device(y, z, x, c) for y in range(4) for z in pair for x in range(4) for c in range(2)] for pair in halves]
+
+
 def send(value, number):
     pairs = []
     for y in range(4):
         for z in range(8):
             for x in range(4):
                 for c in range(2):
-
-                    def at(z):
-                        return (((y * 2 + z // 4) * 4 + x) * 4 + z % 4) * 2 + c
-
-                    pairs.append((at(z), at(TARGETS[number][z])))
+                    pairs.append((device(y, z, x, c), device(y, TARGETS[number][z], x, c)))
     return lax.ppermute(value, AXES, pairs)
 
 
@@ -39,38 +44,14 @@
     return high, (value - high.astype(jnp.float32)).astype(jnp.bfloat16)
 
 
-def pack_kernel(z_ref, core_ref, field_ref, packed_ref, sems):
-    del core_ref
-    first = 1 - (z_ref[0] // 4 ^ z_ref[0] // 2 % 2)
-    copies = [
-        pltpu.make_async_copy(field_ref.at[:, first ^ zn, :, c], packed_ref.at[:, :, zn, c], sems.at[2 * zn + c])
-        for zn in range(2)
-        for c in range(2)
-    ]
-    for copy in copies:
-        copy.start()
-    for copy in copies:
-        copy.wait()
-
-
-def pack(z, core, field):
-    return pl.pallas_call(
-        pack_kernel,
-        in_specs=[SMEM, SMEM, pl.BlockSpec(memory_space=pl.ANY)],
-        out_specs=VMEM,
-        out_shape=f32((4, 4, 2, 2, 4, 32, 128)),
-        scratch_shapes=[pltpu.SemaphoreType.DMA((4,))],
-        compiler_params=params(),
-    )(z, core, field)
-
-
 def contract_kernel(z_ref, core_ref, x_ref, one_ref, two_ref, out_ref, reduced_ref):
     z, core = z_ref[0], core_ref[0]
+    first = 1 - (z // 4 ^ z // 2 % 2)
     high, low = split(one_ref[:, z // 4].reshape(512, 256).T)
     one = jnp.concatenate([high, high, low], axis=1)
     for t in range(4):
-        block = jnp.concatenate([x_ref[:, q, t].reshape(512, 128) for q in range(4)], axis=1)
-        high, low = split(block)
+        block = [x_ref[:, first ^ zn, :, c, t].reshape(512, 128) for zn in range(2) for c in range(2)]
+        high, low = split(jnp.concatenate(block, axis=1))
         high, low = split(dot(one, jnp.concatenate([high, low, high], axis=0)))
         reduced_ref[t] = jnp.concatenate([high, low, high], axis=1)
     high, low = split(two_ref[pl.ds(pl.multiple_of(z // 2 % 2 * 512, 512), 512)])
@@ -120,9 +101,9 @@
 def on_device(species_field, basis_one, basis_two):
     z = sum(lax.axis_index(axis) * size for axis, size in (("zh", 4), ("zp", 2), ("zn", 1))).astype(jnp.int32).reshape(1)
     core = lax.axis_index("c").astype(jnp.int32).reshape(1)
-    packed = pack(z, core, species_field.reshape(4, 2, 4, 2, 4, 32, 128))
-    moved = lax.all_to_all(packed.reshape(256, 32, 128), ("y", "x", "zn", "c"), split_axis=0, concat_axis=0, tiled=True)
-    parts = contract(z, core, moved.reshape(16, 4, 4, 32, 128), basis_one, basis_two)
+    field, z_after, core_after = lax.optimization_barrier((species_field, z, core))
+    moved = lax.all_to_all(field, AXES, split_axis=0, concat_axis=0, axis_index_groups=groups(), tiled=True)
+    parts = contract(z_after, core_after, moved.reshape(4, 2, 4, 2, 4, 32, 128), basis_one, basis_two)
     own, other = add([send(parts[number], number) for number in ORDER])
     return finish(core, own, lax.ppermute(other, "c", [(0, 1), (1, 0)]))
 

time: 98.4 us -> 96.8 us (0.984)
  starting transfers between devices: 11.4 us -> 14.3 us
  local copies, waits for them, and re-layouts: 2.3 us -> 0.11 us
  blocking collectives: 62.3 us -> 61.1 us
    ppermute x4, starting transfers between devices: 10.3 us -> 13.2 us  [send(): return lax.ppermute(value, AXES, pairs)]
    unnamed x6 -> x4, local copies, waits for them, and re-layouts: 2.2 us -> 0.01 us
    all_to_all x1, blocking collectives: 62.3 us -> 61.1 us  [on_device(): lax.all_to_all(field, AXES, split_axis=0, concat_axis=0, axis_index_group...]
  transfers between devices with their start and end apart: 5 -> 5, of which waited for: 3 -> 5; matrix products, arithmetic and copies ran while one was open for 0% -> 0% of each run, Pallas kernels for 0% -> 0%
where the time goes in v6:
time: 96.8 us; the launch traced here: 96.6 us
  blocking collectives  61.1 us (63%)
  waiting for transfers between devices  17.6 us (18%)
  starting transfers between devices  14.3 us (15%)
  Pallas kernels  3.49 us (4%)
    all_to_all x1, blocking collectives, on_device(): lax.all_to_all(field, AXES, split_axis=0, concat_axis=0, axis_index_group...  61.1 us
    ppermute x4, waiting for transfers between devices, send(): return lax.ppermute(value, AXES, pairs)  16.7 us
    ppermute x4, starting transfers between devices, send(): return lax.ppermute(value, AXES, pairs)  13.2 us
    pallas_call x1, Pallas kernels, contract(): pl.pallas_call(contract_kernel, in_specs=[SMEM] * 2 + [VMEM] * 3, out_spe...  2.72 us
  transfers between devices with their start and end apart: 5, of which 5 were waited for; matrix products, arithmetic and copies ran while one was open for 0% of the time, Pallas kernels for 0%

profile of v6, /device:TPU:1, one launch (start us, length us, event | category | flops | bytes accessed | tf_op | source)
XLA Modules:
  0.0 96.6 jit_solution(3444167208707311842)
XLA Ops:
  0.0 0.0 copy-start
  0.0 0.0 copy-start.1
  0.0 61.1 %all_to_all.5 = f32[256,32,128]{2,1,0:T(8,128)S(1)} all-to-all(f32[256,32,128]{2,1,0:T(8,128)} %param.3), channel_id=1, replica_groups={{2,3,10,11,18,19,26,27,0,1,8,9,16,17,24,25,66,67,74,75,82,83,90,91,64,6..., dimensions={0} | all-to-all | bytes 8388608 | tf_op jit(solution)/shard_map/all_to_all | solution.py:105
  61.1 0.0 copy-done
  61.1 0.0 copy-done.1
  61.1 2.7 %shard_map.37 = f32[4,2,4,32,256]{4,3,2,1,0:T(8,128)S(1)} custom-call(s32[1]{0:T(128)} %bitcast.1.z_ref, s32[1]{0:T(128)} %bitcast.core_ref, f32[4,2,4,2,4,32,128]{6,5,4,3,2,1,0:T(8,128)S(1)} %bitcast.12, f32[4,2,4,32,256]{4,3,2,1,0:T(8,128)S(1)} %bitcast.13, f32[1024,256]{1,0:T(8,128)S(1)} %copy-done.1), custom_call_target="tpu_custom_call" | custom-call | flops 2415919104 | bytes 6291456 | tf_op jit(solution)/shard_map/pallas_call | solution.py:67
  63.8 0.1 slice_bitcast_fusion
  63.9 7.5 %collective-permute-start.3 = (f32[2,4,32,256]{3,2,1,0:T(8,128)S(1)}, f32[2,4,32,256]{3,2,1,0:T(8,128)S(1)}, u32[]{:S(2)}, u32[]{:S(2)}) collective-permute-start(f32[2,4,32,256]{3,2,1,0:T(8,128)S(1)} %get-tuple-element.15), channel_id=1, source_target_pairs={{0,38},{1,39},{8,46},{9,47},{16,54},{17,55},{24,62},{25,63},{2,2},... | collective-permute-start | bytes 786440 | tf_op jit(solution)/shard_map/ppermute | solution.py:39
  71.4 1.4 %collective-permute-start.2 = (f32[2,4,32,256]{3,2,1,0:T(8,128)S(1)}, f32[2,4,32,256]{3,2,1,0:T(8,128)S(1)}, u32[]{:S(2)}, u32[]{:S(2)}) collective-permute-start(f32[2,4,32,256]{3,2,1,0:T(8,128)S(1)} %get-tuple-element.16), channel_id=1, source_target_pairs={{0,32},{1,33},{8,40},{9,41},{16,48},{17,49},{24,56},{25,57},{2,4},... | collective-permute-start | bytes 786440 | tf_op jit(solution)/shard_map/ppermute | solution.py:39
  72.8 0.0 collective-permute-start.1
  72.8 4.3 %collective-permute-start = (f32[2,4,32,256]{3,2,1,0:T(8,128)S(1)}, f32[2,4,32,256]{3,2,1,0:T(8,128)S(1)}, u32[]{:S(2)}, u32[]{:S(2)}) collective-permute-start(f32[2,4,32,256]{3,2,1,0:T(8,128)S(1)} %get-tuple-element.18), channel_id=1, source_target_pairs={{0,36},{1,37},{8,44},{9,45},{16,52},{17,53},{24,60},{25,61},{2,0},... | collective-permute-start | bytes 786440 | tf_op jit(solution)/shard_map/ppermute | solution.py:39
  77.1 5.4 %collective-permute-done.3.d_ref = f32[2,4,32,256]{3,2,1,0:T(8,128)S(1)} collective-permute-done((f32[2,4,32,256]{3,2,1,0:T(8,128)S(1)}, f32[2,4,32,256]{3,2,1,0:T(8,128)S(1)}, u32[]{:S(2)}, u32[]{:S(2)}) %collective-permute-start.3) | collective-permute-done | bytes 262176 | tf_op jit(solution)/shard_map/ppermute | solution.py:39
  82.6 0.4 collective-permute-done.2.c_ref
  82.9 9.6 %collective-permute-done.1.b_ref = f32[2,4,32,256]{3,2,1,0:T(8,128)S(1)} collective-permute-done((f32[2,4,32,256]{3,2,1,0:T(8,128)S(1)}, f32[2,4,32,256]{3,2,1,0:T(8,128)S(1)}, u32[]{:S(2)}, u32[]{:S(2)}) %collective-permute-start.1) | collective-permute-done | bytes 262176 | tf_op jit(solution)/shard_map/ppermute | solution.py:39
  92.5 1.3 %collective-permute-done.a_ref = f32[2,4,32,256]{3,2,1,0:T(8,128)S(1)} collective-permute-done((f32[2,4,32,256]{3,2,1,0:T(8,128)S(1)}, f32[2,4,32,256]{3,2,1,0:T(8,128)S(1)}, u32[]{:S(2)}, u32[]{:S(2)}) %collective-permute-start) | collective-permute-done | bytes 262176 | tf_op jit(solution)/shard_map/ppermute | solution.py:39
  93.8 0.1 shard_map.38
  93.8 1.0 %collective-permute-start.4 = (f32[4,32,256]{2,1,0:T(8,128)S(1)}, f32[4,32,256]{2,1,0:T(8,128)S(1)}, u32[]{:S(2)}, u32[]{:S(2)}) collective-permute-start(f32[4,32,256]{2,1,0:T(8,128)S(1)} %get-tuple-element.14), channel_id=1, source_target_pairs={{0,1},{1,0},{2,3},{3,2},{4,5},{5,4},{6,7},{7,6},{8,9},{9,8},{10,11... | collective-permute-start | bytes 393224 | tf_op jit(solution)/shard_map/ppermute | solution.py:108
  94.9 1.0 %collective-permute-done.4.swapped_ref = f32[4,32,256]{2,1,0:T(8,128)S(1)} collective-permute-done((f32[4,32,256]{2,1,0:T(8,128)S(1)}, f32[4,32,256]{2,1,0:T(8,128)S(1)}, u32[]{:S(2)}, u32[]{:S(2)}) %collective-permute-start.4) | collective-permute-done | bytes 131104 | tf_op jit(solution)/shard_map/ppermute | solution.py:108
  95.9 0.7 shard_map.39
Async XLA Ops:
  0.0 61.1 %copy-start = (f32[1024,256]{1,0:T(8,128)S(1)}, f32[1024,256]{1,0:T(8,128)}, u32[]{:S(2)}) copy-start(f32[1024,256]{1,0:T(8,128)} %param.4) | copy-start | bytes 3145732
  0.0 61.1 %copy-start.1 = (f32[1024,256]{1,0:T(8,128)S(1)}, f32[1024,256]{1,0:T(8,128)}, u32[]{:S(2)}) copy-start(f32[1024,256]{1,0:T(8,128)} %two_ref.1) | copy-start | bytes 3145732
  63.9 18.6 %collective-permute-start.3 = (f32[2,4,32,256]{3,2,1,0:T(8,128)S(1)}, f32[2,4,32,256]{3,2,1,0:T(8,128)S(1)}, u32[]{:S(2)}, u32[]{:S(2)}) collective-permute-start(f32[2,4,32,256]{3,2,1,0:T(8,128)S(1)} %get-tuple-element.15), channel_id=1, source_target_pairs={{0,38},{1,39},{8,46},{9,47},{16,54},{17,55},{24,62},{25,63},{2,2},... | collective-permute-start | bytes 786440 | tf_op jit(solution)/shard_map/ppermute | solution.py:39
  71.4 11.5 %collective-permute-start.2 = (f32[2,4,32,256]{3,2,1,0:T(8,128)S(1)}, f32[2,4,32,256]{3,2,1,0:T(8,128)S(1)}, u32[]{:S(2)}, u32[]{:S(2)}) collective-permute-start(f32[2,4,32,256]{3,2,1,0:T(8,128)S(1)} %get-tuple-element.16), channel_id=1, source_target_pairs={{0,32},{1,33},{8,40},{9,41},{16,48},{17,49},{24,56},{25,57},{2,4},... | collective-permute-start | bytes 786440 | tf_op jit(solution)/shard_map/ppermute | solution.py:39
  72.8 19.7 %collective-permute-start.1 = (f32[2,4,32,256]{3,2,1,0:T(8,128)S(1)}, f32[2,4,32,256]{3,2,1,0:T(8,128)S(1)}, u32[]{:S(2)}, u32[]{:S(2)}) collective-permute-start(f32[2,4,32,256]{3,2,1,0:T(8,128)S(1)} %get-tuple-element.17), channel_id=1, source_target_pairs={{0,34},{1,35},{8,42},{9,43},{16,50},{17,51},{24,58},{25,59},{2,6},... | collective-permute-start | bytes 786440 | tf_op jit(solution)/shard_map/ppermute | solution.py:39
  72.8 21.0 %collective-permute-start = (f32[2,4,32,256]{3,2,1,0:T(8,128)S(1)}, f32[2,4,32,256]{3,2,1,0:T(8,128)S(1)}, u32[]{:S(2)}, u32[]{:S(2)}) collective-permute-start(f32[2,4,32,256]{3,2,1,0:T(8,128)S(1)} %get-tuple-element.18), channel_id=1, source_target_pairs={{0,36},{1,37},{8,44},{9,45},{16,52},{17,53},{24,60},{25,61},{2,0},... | collective-permute-start | bytes 786440 | tf_op jit(solution)/shard_map/ppermute | solution.py:39
  93.8 2.0 %collective-permute-start.4 = (f32[4,32,256]{2,1,0:T(8,128)S(1)}, f32[4,32,256]{2,1,0:T(8,128)S(1)}, u32[]{:S(2)}, u32[]{:S(2)}) collective-permute-start(f32[4,32,256]{2,1,0:T(8,128)S(1)} %get-tuple-element.14), channel_id=1, source_target_pairs={{0,1},{1,0},{2,3},{3,2},{4,5},{5,4},{6,7},{7,6},{8,9},{9,8},{10,11... | collective-permute-start | bytes 393224 | tf_op jit(solution)/shard_map/ppermute | solution.py:108

commit v7 on v6

--- a/solution.py
+++ b/solution.py
@@ -10,9 +10,9 @@
 AXES = ("y", "zh", "x", "zp", "zn", "c")
 SIZES = (4, 2, 4, 2, 2, 2)
 FIRST = (1, 2, 4, 7)
-SENDS = ((1, 2, 3, 0), (0, 3, 2, 1), (2, 1, 0, 3), (3, 0, 1, 2))
+SENDS = ((2, 1, 3, 0), (3, 0, 2, 1), (0, 3, 1, 2), (1, 2, 0, 3))
 TARGETS = [dict(zip(FIRST, to)) | {7 - z: 7 - t for z, t in zip(FIRST, to)} for to in SENDS]
-ORDER = (1, 3, 2, 0)
+ORDER = (1, 2, 3, 0)
 VMEM = pl.BlockSpec(memory_space=pltpu.VMEM)
 SMEM = pl.BlockSpec(memory_space=pltpu.SMEM)
 f32 = functools.partial(jax.ShapeDtypeStruct, dtype=jnp.float32)

time: 96.8 us -> 95.1 us (0.982)
  transfers between devices with their start and end apart: 5 -> 5, of which waited for: 5 -> 4; matrix products, arithmetic and copies ran while one was open for 0% -> 0% of each run, Pallas kernels for 0% -> 0%
where the time goes in v7:
time: 95.1 us; the launch traced here: 94.9 us
  blocking collectives  61.1 us (64%)
  waiting for transfers between devices  16.8 us (18%)
  starting transfers between devices  13.4 us (14%)
  Pallas kernels  3.49 us (4%)
    all_to_all x1, blocking collectives, on_device(): lax.all_to_all(field, AXES, split_axis=0, concat_axis=0, axis_index_group...  61.1 us
    ppermute x4, waiting for transfers between devices, send(): return lax.ppermute(value, AXES, pairs)  15.8 us
    ppermute x4, starting transfers between devices, send(): return lax.ppermute(value, AXES, pairs)  12.8 us
    pallas_call x1, Pallas kernels, contract(): pl.pallas_call(contract_kernel, in_specs=[SMEM] * 2 + [VMEM] * 3, out_spe...  2.72 us
  transfers between devices with their start and end apart: 5, of which 4 were waited for; matrix products, arithmetic and copies ran while one was open for 0% of the time, Pallas kernels for 0%

profile of v7, /device:TPU:1, one launch (start us, length us, event | category | flops | bytes accessed | tf_op | source)
XLA Modules:
  0.0 94.9 jit_solution(2616038335963048979)
XLA Ops:
  0.0 0.0 copy-start
  0.0 0.0 copy-start.1
  0.0 61.1 %all_to_all.5 = f32[256,32,128]{2,1,0:T(8,128)S(1)} all-to-all(f32[256,32,128]{2,1,0:T(8,128)} %param.3), channel_id=1, replica_groups={{2,3,10,11,18,19,26,27,0,1,8,9,16,17,24,25,66,67,74,75,82,83,90,91,64,6..., dimensions={0} | all-to-all | bytes 8388608 | tf_op jit(solution)/shard_map/all_to_all | solution.py:105
  61.1 0.0 copy-done
  61.1 0.0 copy-done.1
  61.1 2.7 %shard_map.37 = f32[4,2,4,32,256]{4,3,2,1,0:T(8,128)S(1)} custom-call(s32[1]{0:T(128)} %bitcast.1.z_ref, s32[1]{0:T(128)} %bitcast.core_ref, f32[4,2,4,2,4,32,128]{6,5,4,3,2,1,0:T(8,128)S(1)} %bitcast.12, f32[4,2,4,32,256]{4,3,2,1,0:T(8,128)S(1)} %bitcast.13, f32[1024,256]{1,0:T(8,128)S(1)} %copy-done.1), custom_call_target="tpu_custom_call" | custom-call | flops 2415919104 | bytes 6291456 | tf_op jit(solution)/shard_map/pallas_call | solution.py:67
  63.8 0.1 slice_bitcast_fusion
  63.9 5.6 %collective-permute-start.3 = (f32[2,4,32,256]{3,2,1,0:T(8,128)S(1)}, f32[2,4,32,256]{3,2,1,0:T(8,128)S(1)}, u32[]{:S(2)}, u32[]{:S(2)}) collective-permute-start(f32[2,4,32,256]{3,2,1,0:T(8,128)S(1)} %get-tuple-element.15), channel_id=1, source_target_pairs={{0,38},{1,39},{8,46},{9,47},{16,54},{17,55},{24,62},{25,63},{2,4},... | collective-permute-start | bytes 786440 | tf_op jit(solution)/shard_map/ppermute | solution.py:39
  69.6 3.3 %collective-permute-start.2 = (f32[2,4,32,256]{3,2,1,0:T(8,128)S(1)}, f32[2,4,32,256]{3,2,1,0:T(8,128)S(1)}, u32[]{:S(2)}, u32[]{:S(2)}) collective-permute-start(f32[2,4,32,256]{3,2,1,0:T(8,128)S(1)} %get-tuple-element.16), channel_id=1, source_target_pairs={{0,32},{1,33},{8,40},{9,41},{16,48},{17,49},{24,56},{25,57},{2,2},... | collective-permute-start | bytes 786440 | tf_op jit(solution)/shard_map/ppermute | solution.py:39
  72.8 0.1 collective-permute-start.1
  72.9 3.8 %collective-permute-start = (f32[2,4,32,256]{3,2,1,0:T(8,128)S(1)}, f32[2,4,32,256]{3,2,1,0:T(8,128)S(1)}, u32[]{:S(2)}, u32[]{:S(2)}) collective-permute-start(f32[2,4,32,256]{3,2,1,0:T(8,128)S(1)} %get-tuple-element.18), channel_id=1, source_target_pairs={{0,36},{1,37},{8,44},{9,45},{16,52},{17,53},{24,60},{25,61},{2,6},... | collective-permute-start | bytes 786440 | tf_op jit(solution)/shard_map/ppermute | solution.py:39
  76.7 0.0 collective-permute-done.3.d_ref
  76.7 6.7 %collective-permute-done.2.c_ref = f32[2,4,32,256]{3,2,1,0:T(8,128)S(1)} collective-permute-done((f32[2,4,32,256]{3,2,1,0:T(8,128)S(1)}, f32[2,4,32,256]{3,2,1,0:T(8,128)S(1)}, u32[]{:S(2)}, u32[]{:S(2)}) %collective-permute-start.2) | collective-permute-done | bytes 262176 | tf_op jit(solution)/shard_map/ppermute | solution.py:39
  83.5 6.2 %collective-permute-done.1.b_ref = f32[2,4,32,256]{3,2,1,0:T(8,128)S(1)} collective-permute-done((f32[2,4,32,256]{3,2,1,0:T(8,128)S(1)}, f32[2,4,32,256]{3,2,1,0:T(8,128)S(1)}, u32[]{:S(2)}, u32[]{:S(2)}) %collective-permute-start.1) | collective-permute-done | bytes 262176 | tf_op jit(solution)/shard_map/ppermute | solution.py:39
  89.7 2.9 %collective-permute-done.a_ref = f32[2,4,32,256]{3,2,1,0:T(8,128)S(1)} collective-permute-done((f32[2,4,32,256]{3,2,1,0:T(8,128)S(1)}, f32[2,4,32,256]{3,2,1,0:T(8,128)S(1)}, u32[]{:S(2)}, u32[]{:S(2)}) %collective-permute-start) | collective-permute-done | bytes 262176 | tf_op jit(solution)/shard_map/ppermute | solution.py:39
  92.5 0.1 shard_map.38
  92.6 0.6 collective-permute-start.4
  93.2 1.0 %collective-permute-done.4.swapped_ref = f32[4,32,256]{2,1,0:T(8,128)S(1)} collective-permute-done((f32[4,32,256]{2,1,0:T(8,128)S(1)}, f32[4,32,256]{2,1,0:T(8,128)S(1)}, u32[]{:S(2)}, u32[]{:S(2)}) %collective-permute-start.4) | collective-permute-done | bytes 131104 | tf_op jit(solution)/shard_map/ppermute | solution.py:108
  94.1 0.7 shard_map.39
Async XLA Ops:
  0.0 61.1 %copy-start = (f32[1024,256]{1,0:T(8,128)S(1)}, f32[1024,256]{1,0:T(8,128)}, u32[]{:S(2)}) copy-start(f32[1024,256]{1,0:T(8,128)} %param.4) | copy-start | bytes 3145732
  0.0 61.1 %copy-start.1 = (f32[1024,256]{1,0:T(8,128)S(1)}, f32[1024,256]{1,0:T(8,128)}, u32[]{:S(2)}) copy-start(f32[1024,256]{1,0:T(8,128)} %two_ref.1) | copy-start | bytes 3145732
  63.9 12.8 %collective-permute-start.3 = (f32[2,4,32,256]{3,2,1,0:T(8,128)S(1)}, f32[2,4,32,256]{3,2,1,0:T(8,128)S(1)}, u32[]{:S(2)}, u32[]{:S(2)}) collective-permute-start(f32[2,4,32,256]{3,2,1,0:T(8,128)S(1)} %get-tuple-element.15), channel_id=1, source_target_pairs={{0,38},{1,39},{8,46},{9,47},{16,54},{17,55},{24,62},{25,63},{2,4},... | collective-permute-start | bytes 786440 | tf_op jit(solution)/shard_map/ppermute | solution.py:39
  69.6 13.9 %collective-permute-start.2 = (f32[2,4,32,256]{3,2,1,0:T(8,128)S(1)}, f32[2,4,32,256]{3,2,1,0:T(8,128)S(1)}, u32[]{:S(2)}, u32[]{:S(2)}) collective-permute-start(f32[2,4,32,256]{3,2,1,0:T(8,128)S(1)} %get-tuple-element.16), channel_id=1, source_target_pairs={{0,32},{1,33},{8,40},{9,41},{16,48},{17,49},{24,56},{25,57},{2,2},... | collective-permute-start | bytes 786440 | tf_op jit(solution)/shard_map/ppermute | solution.py:39
  72.8 16.8 %collective-permute-start.1 = (f32[2,4,32,256]{3,2,1,0:T(8,128)S(1)}, f32[2,4,32,256]{3,2,1,0:T(8,128)S(1)}, u32[]{:S(2)}, u32[]{:S(2)}) collective-permute-start(f32[2,4,32,256]{3,2,1,0:T(8,128)S(1)} %get-tuple-element.17), channel_id=1, source_target_pairs={{0,34},{1,35},{8,42},{9,43},{16,50},{17,51},{24,58},{25,59},{2,0},... | collective-permute-start | bytes 786440 | tf_op jit(solution)/shard_map/ppermute | solution.py:39
  72.9 19.6 %collective-permute-start = (f32[2,4,32,256]{3,2,1,0:T(8,128)S(1)}, f32[2,4,32,256]{3,2,1,0:T(8,128)S(1)}, u32[]{:S(2)}, u32[]{:S(2)}) collective-permute-start(f32[2,4,32,256]{3,2,1,0:T(8,128)S(1)} %get-tuple-element.18), channel_id=1, source_target_pairs={{0,36},{1,37},{8,44},{9,45},{16,52},{17,53},{24,60},{25,61},{2,6},... | collective-permute-start | bytes 786440 | tf_op jit(solution)/shard_map/ppermute | solution.py:39
  92.6 1.6 %collective-permute-start.4 = (f32[4,32,256]{2,1,0:T(8,128)S(1)}, f32[4,32,256]{2,1,0:T(8,128)S(1)}, u32[]{:S(2)}, u32[]{:S(2)}) collective-permute-start(f32[4,32,256]{2,1,0:T(8,128)S(1)} %get-tuple-element.14), channel_id=1, source_target_pairs={{0,1},{1,0},{2,3},{3,2},{4,5},{5,4},{6,7},{7,6},{8,9},{9,8},{10,11... | collective-permute-start | bytes 393224 | tf_op jit(solution)/shard_map/ppermute | solution.py:108

commit v8 on v7

--- a/solution.py
+++ b/solution.py
@@ -48,11 +48,11 @@
     z, core = z_ref[0], core_ref[0]
     first = 1 - (z // 4 ^ z // 2 % 2)
     high, low = split(one_ref[:, z // 4].reshape(512, 256).T)
-    one = jnp.concatenate([high, high, low], axis=1)
+    one_high, one = high, jnp.concatenate([high, low], axis=1)
     for t in range(4):
         block = [x_ref[:, first ^ zn, :, c, t].reshape(512, 128) for zn in range(2) for c in range(2)]
         high, low = split(jnp.concatenate(block, axis=1))
-        high, low = split(dot(one, jnp.concatenate([high, low, high], axis=0)))
+        high, low = split(dot(one, jnp.concatenate([high, high], axis=0)) + dot(one_high, low))
         reduced_ref[t] = jnp.concatenate([high, low, high], axis=1)
     high, low = split(two_ref[pl.ds(pl.multiple_of(z // 2 % 2 * 512, 512), 512)])
     partial = dot(reduced_ref[...].reshape(1024, 1536), jnp.concatenate([high, high, low], axis=0)).reshape(4, 256, 256)

time: 95.1 us -> 95 us (level)
  no operation moved by 1% of the time
where the time goes in v8:
time: 95 us; the launch traced here: 94.8 us
  blocking collectives  61.1 us (64%)
  waiting for transfers between devices  16.8 us (18%)
  starting transfers between devices  13.4 us (14%)
  Pallas kernels  3.44 us (4%)
    all_to_all x1, blocking collectives, on_device(): lax.all_to_all(field, AXES, split_axis=0, concat_axis=0, axis_index_group...  61.1 us
    ppermute x4, waiting for transfers between devices, send(): return lax.ppermute(value, AXES, pairs)  15.8 us
    ppermute x4, starting transfers between devices, send(): return lax.ppermute(value, AXES, pairs)  12.8 us
    pallas_call x1, Pallas kernels, contract(): pl.pallas_call(contract_kernel, in_specs=[SMEM] * 2 + [VMEM] * 3, out_spe...  2.67 us
  transfers between devices with their start and end apart: 5, of which 4 were waited for; matrix products, arithmetic and copies ran while one was open for 0% of the time, Pallas kernels for 0%

profile of v8, /device:TPU:1, one launch (start us, length us, event | category | flops | bytes accessed | tf_op | source)
XLA Modules:
  0.0 94.8 jit_solution(12470479758868216640)
XLA Ops:
  0.0 0.0 copy-start
  0.0 0.0 copy-start.1
  0.0 61.1 %all_to_all.5 = f32[256,32,128]{2,1,0:T(8,128)S(1)} all-to-all(f32[256,32,128]{2,1,0:T(8,128)} %param.3), channel_id=1, replica_groups={{2,3,10,11,18,19,26,27,0,1,8,9,16,17,24,25,66,67,74,75,82,83,90,91,64,6..., dimensions={0} | all-to-all | bytes 8388608 | tf_op jit(solution)/shard_map/all_to_all | solution.py:105
  61.1 0.0 copy-done
  61.1 0.0 copy-done.1
  61.1 2.7 %shard_map.37 = f32[4,2,4,32,256]{4,3,2,1,0:T(8,128)S(1)} custom-call(s32[1]{0:T(128)} %bitcast.1.z_ref, s32[1]{0:T(128)} %bitcast.core_ref, f32[4,2,4,2,4,32,128]{6,5,4,3,2,1,0:T(8,128)S(1)} %bitcast.12, f32[4,2,4,32,256]{4,3,2,1,0:T(8,128)S(1)} %bitcast.13, f32[1024,256]{1,0:T(8,128)S(1)} %copy-done.1), custom_call_target="tpu_custom_call" | custom-call | flops 2415919104 | bytes 6291456 | tf_op jit(solution)/shard_map/pallas_call | solution.py:67
  63.7 0.1 slice_bitcast_fusion
  63.9 5.6 %collective-permute-start.3 = (f32[2,4,32,256]{3,2,1,0:T(8,128)S(1)}, f32[2,4,32,256]{3,2,1,0:T(8,128)S(1)}, u32[]{:S(2)}, u32[]{:S(2)}) collective-permute-start(f32[2,4,32,256]{3,2,1,0:T(8,128)S(1)} %get-tuple-element.15), channel_id=1, source_target_pairs={{0,38},{1,39},{8,46},{9,47},{16,54},{17,55},{24,62},{25,63},{2,4},... | collective-permute-start | bytes 786440 | tf_op jit(solution)/shard_map/ppermute | solution.py:39
  69.5 3.3 %collective-permute-start.2 = (f32[2,4,32,256]{3,2,1,0:T(8,128)S(1)}, f32[2,4,32,256]{3,2,1,0:T(8,128)S(1)}, u32[]{:S(2)}, u32[]{:S(2)}) collective-permute-start(f32[2,4,32,256]{3,2,1,0:T(8,128)S(1)} %get-tuple-element.16), channel_id=1, source_target_pairs={{0,32},{1,33},{8,40},{9,41},{16,48},{17,49},{24,56},{25,57},{2,2},... | collective-permute-start | bytes 786440 | tf_op jit(solution)/shard_map/ppermute | solution.py:39
  72.8 0.1 collective-permute-start.1
  72.9 3.8 %collective-permute-start = (f32[2,4,32,256]{3,2,1,0:T(8,128)S(1)}, f32[2,4,32,256]{3,2,1,0:T(8,128)S(1)}, u32[]{:S(2)}, u32[]{:S(2)}) collective-permute-start(f32[2,4,32,256]{3,2,1,0:T(8,128)S(1)} %get-tuple-element.18), channel_id=1, source_target_pairs={{0,36},{1,37},{8,44},{9,45},{16,52},{17,53},{24,60},{25,61},{2,6},... | collective-permute-start | bytes 786440 | tf_op jit(solution)/shard_map/ppermute | solution.py:39
  76.7 0.0 collective-permute-done.3.d_ref
  76.7 6.7 %collective-permute-done.2.c_ref = f32[2,4,32,256]{3,2,1,0:T(8,128)S(1)} collective-permute-done((f32[2,4,32,256]{3,2,1,0:T(8,128)S(1)}, f32[2,4,32,256]{3,2,1,0:T(8,128)S(1)}, u32[]{:S(2)}, u32[]{:S(2)}) %collective-permute-start.2) | collective-permute-done | bytes 262176 | tf_op jit(solution)/shard_map/ppermute | solution.py:39
  83.4 6.2 %collective-permute-done.1.b_ref = f32[2,4,32,256]{3,2,1,0:T(8,128)S(1)} collective-permute-done((f32[2,4,32,256]{3,2,1,0:T(8,128)S(1)}, f32[2,4,32,256]{3,2,1,0:T(8,128)S(1)}, u32[]{:S(2)}, u32[]{:S(2)}) %collective-permute-start.1) | collective-permute-done | bytes 262176 | tf_op jit(solution)/shard_map/ppermute | solution.py:39
  89.6 2.8 %collective-permute-done.a_ref = f32[2,4,32,256]{3,2,1,0:T(8,128)S(1)} collective-permute-done((f32[2,4,32,256]{3,2,1,0:T(8,128)S(1)}, f32[2,4,32,256]{3,2,1,0:T(8,128)S(1)}, u32[]{:S(2)}, u32[]{:S(2)}) %collective-permute-start) | collective-permute-done | bytes 262176 | tf_op jit(solution)/shard_map/ppermute | solution.py:39
  92.5 0.1 shard_map.38
  92.5 0.6 collective-permute-start.4
  93.1 1.0 %collective-permute-done.4.swapped_ref = f32[4,32,256]{2,1,0:T(8,128)S(1)} collective-permute-done((f32[4,32,256]{2,1,0:T(8,128)S(1)}, f32[4,32,256]{2,1,0:T(8,128)S(1)}, u32[]{:S(2)}, u32[]{:S(2)}) %collective-permute-start.4) | collective-permute-done | bytes 131104 | tf_op jit(solution)/shard_map/ppermute | solution.py:108
  94.1 0.7 shard_map.39
Async XLA Ops:
  0.0 61.1 %copy-start = (f32[1024,256]{1,0:T(8,128)S(1)}, f32[1024,256]{1,0:T(8,128)}, u32[]{:S(2)}) copy-start(f32[1024,256]{1,0:T(8,128)} %param.4) | copy-start | bytes 3145732
  0.0 61.1 %copy-start.1 = (f32[1024,256]{1,0:T(8,128)S(1)}, f32[1024,256]{1,0:T(8,128)}, u32[]{:S(2)}) copy-start(f32[1024,256]{1,0:T(8,128)} %two_ref.1) | copy-start | bytes 3145732
  63.9 12.8 %collective-permute-start.3 = (f32[2,4,32,256]{3,2,1,0:T(8,128)S(1)}, f32[2,4,32,256]{3,2,1,0:T(8,128)S(1)}, u32[]{:S(2)}, u32[]{:S(2)}) collective-permute-start(f32[2,4,32,256]{3,2,1,0:T(8,128)S(1)} %get-tuple-element.15), channel_id=1, source_target_pairs={{0,38},{1,39},{8,46},{9,47},{16,54},{17,55},{24,62},{25,63},{2,4},... | collective-permute-start | bytes 786440 | tf_op jit(solution)/shard_map/ppermute | solution.py:39
  69.5 13.9 %collective-permute-start.2 = (f32[2,4,32,256]{3,2,1,0:T(8,128)S(1)}, f32[2,4,32,256]{3,2,1,0:T(8,128)S(1)}, u32[]{:S(2)}, u32[]{:S(2)}) collective-permute-start(f32[2,4,32,256]{3,2,1,0:T(8,128)S(1)} %get-tuple-element.16), channel_id=1, source_target_pairs={{0,32},{1,33},{8,40},{9,41},{16,48},{17,49},{24,56},{25,57},{2,2},... | collective-permute-start | bytes 786440 | tf_op jit(solution)/shard_map/ppermute | solution.py:39
  72.8 16.9 %collective-permute-start.1 = (f32[2,4,32,256]{3,2,1,0:T(8,128)S(1)}, f32[2,4,32,256]{3,2,1,0:T(8,128)S(1)}, u32[]{:S(2)}, u32[]{:S(2)}) collective-permute-start(f32[2,4,32,256]{3,2,1,0:T(8,128)S(1)} %get-tuple-element.17), channel_id=1, source_target_pairs={{0,34},{1,35},{8,42},{9,43},{16,50},{17,51},{24,58},{25,59},{2,0},... | collective-permute-start | bytes 786440 | tf_op jit(solution)/shard_map/ppermute | solution.py:39
  72.9 19.6 %collective-permute-start = (f32[2,4,32,256]{3,2,1,0:T(8,128)S(1)}, f32[2,4,32,256]{3,2,1,0:T(8,128)S(1)}, u32[]{:S(2)}, u32[]{:S(2)}) collective-permute-start(f32[2,4,32,256]{3,2,1,0:T(8,128)S(1)} %get-tuple-element.18), channel_id=1, source_target_pairs={{0,36},{1,37},{8,44},{9,45},{16,52},{17,53},{24,60},{25,61},{2,6},... | collective-permute-start | bytes 786440 | tf_op jit(solution)/shard_map/ppermute | solution.py:39
  92.5 1.6 %collective-permute-start.4 = (f32[4,32,256]{2,1,0:T(8,128)S(1)}, f32[4,32,256]{2,1,0:T(8,128)S(1)}, u32[]{:S(2)}, u32[]{:S(2)}) collective-permute-start(f32[4,32,256]{2,1,0:T(8,128)S(1)} %get-tuple-element.14), channel_id=1, source_target_pairs={{0,1},{1,0},{2,3},{3,2},{4,5},{5,4},{6,7},{7,6},{8,9},{9,8},{10,11... | collective-permute-start | bytes 393224 | tf_op jit(solution)/shard_map/ppermute | solution.py:108
